TPU v7x, 512 devices: a whole 4x8x8 slice. The times are simulated.
512 devices in a mesh: dp: 64 (over y, z), mp: 8 (over x, core).
Axes of the slice: x: 4, y: 8, z: 8, core: 2. Of those that a mesh axis runs over, the one named last changes fastest.
Arguments:
- activations: bfloat16 [8192, 5120], P('dp'), may hold values from -6 to 6
- cotangent: bfloat16 [8192, 17408], P('dp', 'mp'), may hold values from -6 to 6
- error_sketch: float32 [8, 2, 8, 16384], P('mp', None, None, 'dp'), may hold values from -24 to 24
- buckets: int32 [2, 40, 136], P(None, None, 'mp'), may hold values from 0 to 7
- sign_bits: int32 [2, 40, 136], P(None, None, 'mp'), may hold values from 0 to 1
- heavy_blocks: int32 [64], P('mp'), may hold values from 0 to 679
Outputs:
- update: float32 [8, 8, 16384], P('mp', None, 'dp')
- new_error: float32 [8, 2, 8, 16384], P('mp', None, None, 'dp')
Inputs may be any that keep to these rules, and one draw needn't show every extreme that they name: `heavy_blocks`: block numbers are local to a hidden-unit shard: row block times 17408 / 1024 plus column block; repeats may occur.
All inputs are finite; a program needn't handle non-finite values.
Results may differ from a plain program's by a relative error of at most 0.0003.
Values sent between devices are 32-bit elements; how exact they have to be, the bound alone decides.
No kernel may reach another device: no remote copies, remote signals or barrier semaphores. Data moves between devices by JAX's collectives and lax.ppermute only.
A program may use at most 64 MiB of HBM per device.

v0:
```python
import jax
import jax.numpy as jnp
from jax import lax
from jax.sharding import PartitionSpec as P

ROWS = 2
BUCKETS = 8
HEAVY = 8


def body(activations, cotangent, error_sketch, buckets, sign_bits, heavy_blocks):
    high = lax.Precision.HIGHEST
    tok_rows, width_d = activations.shape
    width = cotangent.shape[1]
    block = 128
    cells = block * block
    col_blocks = width // block
    row_blocks = width_d // block
    group = 1024
    group_blocks = group // block
    groups = width_d // group
    inverse = 1.0 / tok_rows
    bucket_ids = jnp.arange(BUCKETS, dtype=jnp.int32)
    piece = error_sketch.shape[3]
    offset = lax.axis_index("dp") * piece
    sketch_rows = ROWS * BUCKETS
    bucket_flat = buckets.reshape(ROWS, row_blocks * col_blocks)
    sign_flat = (2 * sign_bits - 1).reshape(ROWS, row_blocks * col_blocks).astype(jnp.float32)
    sketch_map = (bucket_flat[:, None, :] == bucket_ids[None, :, None]).astype(
        jnp.float32
    ) * sign_flat[:, None, :]
    sketch_map = sketch_map.reshape(ROWS, BUCKETS, row_blocks, col_blocks)
    heavy_row = heavy_blocks // col_blocks
    heavy_col = heavy_blocks % col_blocks
    heavy_bucket = jnp.take(bucket_flat, heavy_blocks, axis=1)
    heavy_sign = jnp.take(sign_flat, heavy_blocks, axis=1)
    picks = (heavy_bucket[:, :, None] == bucket_ids[None, None, :]).astype(
        jnp.float32
    ) * heavy_sign[:, :, None]
    cot_blocks = cotangent.astype(jnp.float32).reshape(tok_rows, col_blocks, block)

    def add_group(index, total):
        act_cols = (
            lax.dynamic_slice_in_dim(activations, index * group, group, 1)
            .astype(jnp.float32)
            .reshape(tok_rows, group_blocks, block)
        )
        map_part = lax.dynamic_slice_in_dim(sketch_map, index * group_blocks, group_blocks, 2)
        weighted = jnp.einsum("rbac,tcq->tarbq", map_part, cot_blocks, precision=high).reshape(
            tok_rows, group_blocks, sketch_rows * block
        )
        return total + lax.dot_general(
            act_cols, weighted, (((0, 1), (0, 1)), ((), ())), precision=high
        )

    folded = lax.fori_loop(
        0, groups, add_group, jnp.zeros((block, sketch_rows * block), jnp.float32)
    )
    sketch_local = (folded.reshape(block, sketch_rows, block).transpose(1, 0, 2) * inverse).reshape(
        ROWS, BUCKETS, cells
    )
    act_pick = jnp.take(activations.reshape(tok_rows, row_blocks, block), heavy_row, axis=1)
    cot_pick = jnp.take(cotangent.reshape(tok_rows, col_blocks, block), heavy_col, axis=1)
    local = (
        jnp.einsum("tkp,tkq->kpq", act_pick, cot_pick, preferred_element_type=jnp.float32) * inverse
    )
    local = local.reshape(HEAVY, cells)
    summed = lax.psum(local, "dp")
    exact = lax.dynamic_slice_in_dim(summed, offset, piece, 1)
    summed = lax.psum(sketch_local, "dp")
    sketch = lax.dynamic_slice_in_dim(summed, offset, piece, 2)
    error_part = error_sketch[0]
    estimate = jnp.einsum("rkb,rbe->ke", picks, error_part, precision=high) * (1.0 / ROWS)
    update = estimate + exact
    new_error = error_part + sketch - jnp.einsum("rkb,ke->rbe", picks, update, precision=high)
    return (update[None], new_error[None])


def solution(mesh):
    return jax.shard_map(
        body,
        mesh=mesh,
        in_specs=(
            P("dp", None),
            P("dp", "mp"),
            P("mp", None, None, "dp"),
            P(None, None, "mp"),
            P(None, None, "mp"),
            P("mp"),
        ),
        out_specs=(P("mp", None, "dp"), P("mp", None, None, "dp")),
        check_vma=False,
    )
```

profile of v0, /device:TPU:6, one launch (start us, length us, event | category | flops | bytes accessed | tf_op | source)
XLA Modules:
  0.0 329.3 jit_solution(9047948445347468019)
XLA Ops:
  7.2 0.0 all-reduce.3.cloned.1.call-start
  7.2 1.4 copy.47
  8.6 0.0 copy-start.5
  8.6 0.0 copy-start.3
  8.6 0.0 copy-start.4
  8.6 1.1 copy.48
  9.7 0.4 copy.53
  10.1 0.0 copy-done.5
  10.1 0.0 copy-done.3
  10.2 0.1 copy.41
  10.2 0.0 copy-done.4
  10.2 0.1 copy.38
  10.3 2.4 copy.45
  12.8 134.4 %while.14 = (s32[]{:T(128)}, f32[128,2048]{1,0:T(8,128)S(1)}, bf16[128,5120]{0,1:T(8,128)(2,1)}, f32[2,8,40,17]{3,2,1,0:T(8,128)S(1)}, f32[128,17,128]{2,1,0:T(8...) while((s32[]{:T(128)}, f32[128,2048]{1,0:T(8,128)S(1)}, ...), condition=%wide.region_2.3_spmd.clone, body=%wide.region_1.2_spmd.clone.sunk | while | flops 3649568768 | bytes 38076640 | solution.py:56
  12.8 1.0 constant_dynamic-slice_fusion.2
  13.8 8.8 %convolution_bitcast_fusion.4 = f32[128,8,2,8,128]{4,1,0,3,2:T(8,128)} fusion(f32[128,17,128]{2,1,0:T(8,128)S(1)} %get-tuple-element.208, f32[2,8,40,17]{3,2,1,0:T(8,128)S(1)} %get-tuple-element.207, s32[]{:T(128)S(6)} %select_n.112), kind=kOutput, calls=%fused_computation.4.clone.1 | convolution fusion | flops 427819008 | bytes 10027012 | tf_op jit(solution)/shard_map/while/body/eval_jaxpr/rbac,tcq->tarbq/dot_general | solution.py:49
  22.6 8.7 %copy.66 = f32[128,8,2,8,128]{0,4,3,2,1:T(8,128)} copy(f32[128,8,2,8,128]{4,1,0,3,2:T(8,128)} %convolution_bitcast_fusion.4) | data formatting | bytes 16777216 | tf_op jit(solution)/shard_map/while/body/eval_jaxpr/rbac,tcq->tarbq/transpose | solution.py:49
  31.2 8.4 %fusion.41 = f32[128,2048]{1,0:T(8,128)S(1)} fusion(bf16[128,8,128]{0,2,1:T(8,128)(2,1)S(1)} %bitcast.79, f32[128,8,2048]{0,2,1:T(8,128)} %bitcast.78, f32[128,2048]{1,0:T(8,128)S(1)} %get-tuple-element.194, pred[]{:T(512)S(6)} %compare.3), kind=kOutput, calls=%fused_computation.6.clone.1 | convolution fusion | flops 3221749760 | bytes 10747905 | tf_op jit(solution)/shard_map/while/body/eval_jaxpr/dot_general | solution.py:52
  39.7 1.0 constant_dynamic-slice_fusion.2
  40.7 8.8 %convolution_bitcast_fusion.4 = f32[128,8,2,8,128]{4,1,0,3,2:T(8,128)} fusion(f32[128,17,128]{2,1,0:T(8,128)S(1)} %get-tuple-element.208, f32[2,8,40,17]{3,2,1,0:T(8,128)S(1)} %get-tuple-element.207, s32[]{:T(128)S(6)} %select_n.112), kind=kOutput, calls=%fused_computation.4.clone.1 | convolution fusion | flops 427819008 | bytes 10027012 | tf_op jit(solution)/shard_map/while/body/eval_jaxpr/rbac,tcq->tarbq/dot_general | solution.py:49
  49.5 8.7 %copy.66 = f32[128,8,2,8,128]{0,4,3,2,1:T(8,128)} copy(f32[128,8,2,8,128]{4,1,0,3,2:T(8,128)} %convolution_bitcast_fusion.4) | data formatting | bytes 16777216 | tf_op jit(solution)/shard_map/while/body/eval_jaxpr/rbac,tcq->tarbq/transpose | solution.py:49
  58.1 8.4 %fusion.41 = f32[128,2048]{1,0:T(8,128)S(1)} fusion(bf16[128,8,128]{0,2,1:T(8,128)(2,1)S(1)} %bitcast.79, f32[128,8,2048]{0,2,1:T(8,128)} %bitcast.78, f32[128,2048]{1,0:T(8,128)S(1)} %get-tuple-element.194, pred[]{:T(512)S(6)} %compare.3), kind=kOutput, calls=%fused_computation.6.clone.1 | convolution fusion | flops 3221749760 | bytes 10747905 | tf_op jit(solution)/shard_map/while/body/eval_jaxpr/dot_general | solution.py:52
  66.6 1.0 constant_dynamic-slice_fusion.2
  67.6 8.8 %convolution_bitcast_fusion.4 = f32[128,8,2,8,128]{4,1,0,3,2:T(8,128)} fusion(f32[128,17,128]{2,1,0:T(8,128)S(1)} %get-tuple-element.208, f32[2,8,40,17]{3,2,1,0:T(8,128)S(1)} %get-tuple-element.207, s32[]{:T(128)S(6)} %select_n.112), kind=kOutput, calls=%fused_computation.4.clone.1 | convolution fusion | flops 427819008 | bytes 10027012 | tf_op jit(solution)/shard_map/while/body/eval_jaxpr/rbac,tcq->tarbq/dot_general | solution.py:49
  76.4 8.7 %copy.66 = f32[128,8,2,8,128]{0,4,3,2,1:T(8,128)} copy(f32[128,8,2,8,128]{4,1,0,3,2:T(8,128)} %convolution_bitcast_fusion.4) | data formatting | bytes 16777216 | tf_op jit(solution)/shard_map/while/body/eval_jaxpr/rbac,tcq->tarbq/transpose | solution.py:49
  85.0 8.4 %fusion.41 = f32[128,2048]{1,0:T(8,128)S(1)} fusion(bf16[128,8,128]{0,2,1:T(8,128)(2,1)S(1)} %bitcast.79, f32[128,8,2048]{0,2,1:T(8,128)} %bitcast.78, f32[128,2048]{1,0:T(8,128)S(1)} %get-tuple-element.194, pred[]{:T(512)S(6)} %compare.3), kind=kOutput, calls=%fused_computation.6.clone.1 | convolution fusion | flops 3221749760 | bytes 10747905 | tf_op jit(solution)/shard_map/while/body/eval_jaxpr/dot_general | solution.py:52
  93.5 1.0 constant_dynamic-slice_fusion.2
  94.5 8.8 %convolution_bitcast_fusion.4 = f32[128,8,2,8,128]{4,1,0,3,2:T(8,128)} fusion(f32[128,17,128]{2,1,0:T(8,128)S(1)} %get-tuple-element.208, f32[2,8,40,17]{3,2,1,0:T(8,128)S(1)} %get-tuple-element.207, s32[]{:T(128)S(6)} %select_n.112), kind=kOutput, calls=%fused_computation.4.clone.1 | convolution fusion | flops 427819008 | bytes 10027012 | tf_op jit(solution)/shard_map/while/body/eval_jaxpr/rbac,tcq->tarbq/dot_general | solution.py:49
  103.2 8.7 %copy.66 = f32[128,8,2,8,128]{0,4,3,2,1:T(8,128)} copy(f32[128,8,2,8,128]{4,1,0,3,2:T(8,128)} %convolution_bitcast_fusion.4) | data formatting | bytes 16777216 | tf_op jit(solution)/shard_map/while/body/eval_jaxpr/rbac,tcq->tarbq/transpose | solution.py:49
  111.9 8.4 %fusion.41 = f32[128,2048]{1,0:T(8,128)S(1)} fusion(bf16[128,8,128]{0,2,1:T(8,128)(2,1)S(1)} %bitcast.79, f32[128,8,2048]{0,2,1:T(8,128)} %bitcast.78, f32[128,2048]{1,0:T(8,128)S(1)} %get-tuple-element.194, pred[]{:T(512)S(6)} %compare.3), kind=kOutput, calls=%fused_computation.6.clone.1 | convolution fusion | flops 3221749760 | bytes 10747905 | tf_op jit(solution)/shard_map/while/body/eval_jaxpr/dot_general | solution.py:52
  120.4 1.0 constant_dynamic-slice_fusion.2
  121.3 8.8 %convolution_bitcast_fusion.4 = f32[128,8,2,8,128]{4,1,0,3,2:T(8,128)} fusion(f32[128,17,128]{2,1,0:T(8,128)S(1)} %get-tuple-element.208, f32[2,8,40,17]{3,2,1,0:T(8,128)S(1)} %get-tuple-element.207, s32[]{:T(128)S(6)} %select_n.112), kind=kOutput, calls=%fused_computation.4.clone.1 | convolution fusion | flops 427819008 | bytes 10027012 | tf_op jit(solution)/shard_map/while/body/eval_jaxpr/rbac,tcq->tarbq/dot_general | solution.py:49
  130.1 8.7 %copy.66 = f32[128,8,2,8,128]{0,4,3,2,1:T(8,128)} copy(f32[128,8,2,8,128]{4,1,0,3,2:T(8,128)} %convolution_bitcast_fusion.4) | data formatting | bytes 16777216 | tf_op jit(solution)/shard_map/while/body/eval_jaxpr/rbac,tcq->tarbq/transpose | solution.py:49
  138.8 8.4 %fusion.41 = f32[128,2048]{1,0:T(8,128)S(1)} fusion(bf16[128,8,128]{0,2,1:T(8,128)(2,1)S(1)} %bitcast.79, f32[128,8,2048]{0,2,1:T(8,128)} %bitcast.78, f32[128,2048]{1,0:T(8,128)S(1)} %get-tuple-element.194, pred[]{:T(512)S(6)} %compare.3), kind=kOutput, calls=%fused_computation.6.clone.1 | convolution fusion | flops 3221749760 | bytes 10747905 | tf_op jit(solution)/shard_map/while/body/eval_jaxpr/dot_general | solution.py:52
  147.2 0.1 bitcast_bitcast_fusion
  147.4 0.0 copy-start
  147.4 1.2 reshape.95
  148.5 0.5 copy-done
  149.0 0.8 copy.46
  149.8 1.6 gather_fusion.3
  151.5 0.6 gather_fusion.2
  152.1 0.4 fusion.5
  152.5 0.0 copy-start.1
  152.5 1.1 copy.64
  153.6 0.0 all-reduce.3.cloned.1.call-update
  153.6 0.1 convert_element_type.17
  153.7 0.1 reshape.90
  153.9 0.2 copy.39
  154.1 0.6 gather_fusion
  154.6 0.1 select_bitcast_fusion.1
  154.7 0.1 copy.40
  154.8 0.2 copy.42
  155.0 0.6 gather_fusion.1
  155.5 0.1 select_bitcast_fusion
  155.6 0.1 copy.43
  155.7 164.4 %all-reduce.3.cloned.1.call-done = (f32[8,16384]{1,0:T(8,128)}, f32[2,8,16384]{2,1,0:T(8,128)}) async-done(((f32[8,16384]{1,0:T(8,128)}, f32[2,8,16384]{2,1,0:T(8,128)}), (f32[8,16384]{1,0:T(8,128)}, f32[2,8,16384]{2,1,0:T(8,128)})) %all-reduce.3.cloned.1.call-update) | async-done | bytes 1572880 | tf_op jit(solution)/shard_map/psum | solution.py:68
  320.1 0.0 copy-done.1
  320.1 0.9 fusion.8
  321.0 0.0 copy-start.2
  321.0 1.5 fusion.6
  322.5 0.0 copy-done.2
  (7 shorter events, 0.1 us)
Async XLA Ops:
  7.2 312.9 %all-reduce.3.cloned.1.call-start = ((), (), s32[]{:S(2)}) async-start(), calls=%async_computation | async-start | bytes 3145728 | tf_op jit(solution)/shard_map/psum | solution.py:68
  8.6 1.5 copy-start.5
  8.6 1.6 copy-start.3
  8.6 1.7 copy-start.4
  147.4 1.7 copy-start
  152.5 167.6 %copy-start.1 = (f32[1,2,8,256]{3,2,1,0:T(8,128)S(1)}, f32[1,2,8,256]{3,2,1,0:T(8,128)}, u32[]{:S(2)}) copy-start(f32[1,2,8,256]{3,2,1,0:T(8,128)} %param.10) | copy-start | bytes 49156
  321.0 1.5 copy-start.2
Sparse Core Ops, SparseCore 0:
  153.7 166.2 all-reduce.2
where the time goes:
time: 331 us; the launch traced here: 329 us
  waiting for transfers between devices  164 us (50%)
  matrix products  88.8 us (27%)
  local copies, waits for them, and re-layouts  61.4 us (19%)
  between operations  14.2 us (4%)
    psum x1, waiting for transfers between devices, body(): summed = lax.psum(local, 'dp')  164 us
    dot_general x5, matrix products, add_group(): jnp.einsum('rbac,tcq->tarbq', map_part, cot_blocks, precision=high)  43.9 us
    transpose x5, local copies, waits for them, and re-layouts, add_group(): jnp.einsum('rbac,tcq->tarbq', map_part, cot_blocks, precision=high)  43.3 us
    dot_general x5, matrix products, add_group(): lax.dot_general(act_cols, weighted, (((0, 1), (0, 1)), ((), ())), precisi...  42.2 us
  transfers between devices with their start and end apart: 1, of which 1 were waited for; matrix products, arithmetic and copies ran while one was open for 1% of the time, Pallas kernels for 0%

commit v1 on v0

v1 whole, which is shorter than its diff:
```python
import functools
import jax
import jax.numpy as jnp
from jax import lax
from jax.experimental import pallas as pl
from jax.experimental.pallas import tpu as pltpu
from jax.sharding import PartitionSpec as P

ROWS = 2
BUCKETS = 8
HEAVY = 8
BLK = 128
TOK = 128
ROW_BLOCKS = 40
COL_BLOCKS = 17
CPAD = 18
GRP = 4
GROUPS = TOK // GRP
KIN = GRP * ROW_BLOCKS
KC = GRP * CPAD
SKETCH = ROWS * BUCKETS
OUT_ROWS = HEAVY + SKETCH
DEPTH = GROUPS * KC
TN = (((0,), (0,)), ((), ()))
F32 = jnp.float32
BF16 = jnp.bfloat16
RBG = 4
UNROLL = 2
SIDE = 8
NEAR = [[(2 * a + i) * SIDE + 2 * b + j for i in range(2) for j in range(2)] for a in range(4) for b in range(4)]
FAR = [[(2 * a + i) * SIDE + 2 * b + j for a in range(4) for b in range(4)] for i in range(2) for j in range(2)]


def iota(shape, dim):
    return lax.broadcasted_iota(jnp.int32, shape, dim)


def place(p):
    dp = p // 2
    y, z = dp // SIDE, dp % SIDE
    return (((y % 2) * 2 + z % 2) * 16 + (y // 2) * 4 + z // 2) * 2 + p % 2


def kernel(act, cot, bkt, sgn, err, heavy, bkt_s, sgn_s, where, out, act3, cot3, maps, hi, lo, pick):
    perm = (place(iota((BLK, BLK), 0)) == iota((BLK, BLK), 1)).astype(BF16)
    for a in range(ROW_BLOCKS):
        act3[pl.ds(a, TOK, stride=ROW_BLOCKS), :] = jnp.dot(
            act[:, a * BLK : (a + 1) * BLK], perm, preferred_element_type=F32
        )
    for c in range(COL_BLOCKS):
        cot3[pl.ds(c, TOK, stride=CPAD), :] = cot[:, c * BLK : (c + 1) * BLK].astype(F32)
    cot3[pl.ds(COL_BLOCKS, TOK, stride=CPAD), :] = jnp.zeros((TOK, BLK), F32)

    spread_rows = (iota((KC, COL_BLOCKS), 0) % CPAD == iota((KC, COL_BLOCKS), 1)).astype(F32)
    spread_cols = (iota((ROW_BLOCKS, KIN), 1) % ROW_BLOCKS == iota((ROW_BLOCKS, KIN), 0)).astype(F32)
    own = (iota((KC, KIN), 0) // CPAD == iota((KC, KIN), 1) // ROW_BLOCKS) & (
        iota((KC, KIN), 0) % CPAD < COL_BLOCKS
    )
    for r in range(ROWS):
        codes = (bkt[:, r, :] + BUCKETS * sgn[:, r, :]).astype(F32)
        table = jnp.dot(
            jnp.dot(spread_rows, codes, preferred_element_type=F32), spread_cols, preferred_element_type=F32
        )
        table = jnp.where(own, table, -1.0)
        for b in range(0, BUCKETS, 2):
            two = []
            for bb in (b, b + 1):
                plus = (table == bb + BUCKETS).astype(F32)
                minus = (table == bb).astype(F32)
                two.append(plus - minus)
            at = (r * BUCKETS + b) * KC
            maps[at : at + 2 * KC, :] = jnp.concatenate(two, axis=0).astype(BF16)

    def weigh(i, carry):
        first = pl.multiple_of(i * 2 * KIN, 2 * KIN)
        rhs = jnp.concatenate(
            [act3[pl.ds(first, KIN), :], act3[pl.ds(first + KIN, KIN), :]], axis=1
        ).astype(BF16)
        rows = pl.ds(pl.multiple_of(i * 2 * KC, 2 * KC), 2 * KC)
        for g in range(0, SKETCH, RBG):
            many = jnp.dot(maps[g * KC : (g + RBG) * KC, :], rhs, preferred_element_type=F32)
            for j in range(RBG):
                w = many[j * KC : (j + 1) * KC]
                w = jnp.concatenate([w[:, :BLK], w[:, BLK:]], axis=0)
                top = w.astype(BF16)
                cols = slice((g + j) * BLK, (g + j + 1) * BLK)
                hi[rows, cols] = top
                lo[rows, cols] = (w - top.astype(F32)).astype(BF16)
        return carry

    lax.fori_loop(0, GROUPS // 2, weigh, 0, unroll=UNROLL)

    inverse = 1.0 / TOK
    for k in range(HEAVY):
        a = lax.div(heavy[k], COL_BLOCKS)
        c = lax.rem(heavy[k], COL_BLOCKS)
        block = lax.dot_general(
            act3[pl.ds(a, TOK, stride=ROW_BLOCKS), :].astype(BF16),
            cot[:, pl.ds(pl.multiple_of(c * BLK, BLK), BLK)],
            TN,
            preferred_element_type=F32,
        ) * inverse
        pick[k] = block
        out[pl.ds(k, BLK, stride=OUT_ROWS), :] = block

    lhs = cot3[...].T.astype(BF16)
    for rb in range(0, SKETCH, 2):
        cols = slice(rb * BLK, (rb + 2) * BLK)
        total = jnp.dot(lhs, hi[:, cols], preferred_element_type=F32) + jnp.dot(
            lhs, lo[:, cols], preferred_element_type=F32
        )
        for j in range(2):
            out[pl.ds(HEAVY + rb + j, BLK, stride=OUT_ROWS), :] = total[:, j * BLK : (j + 1) * BLK].T * inverse

    mine = place(2 * where[0]) * OUT_ROWS
    for k in range(HEAVY):
        a = lax.div(heavy[k], COL_BLOCKS)
        c = lax.rem(heavy[k], COL_BLOCKS)
        signs = [(2 * sgn_s[c, r, a] - 1).astype(F32) for r in range(ROWS)]
        rows = [r * BUCKETS + bkt_s[c, r, a] for r in range(ROWS)]
        for r in range(ROWS):
            at = pl.ds(HEAVY + rows[r], BLK, stride=OUT_ROWS)
            out[at, :] = out[at, :] - signs[r] * pick[k]
        for j in range(2):
            first = mine + j * OUT_ROWS
            guess = jnp.zeros((1, BLK), F32)
            for r in range(ROWS):
                guess = guess + signs[r] * err[pl.ds(j * SKETCH + rows[r], 1), :]
            guess = guess * (1.0 / ROWS)
            out[pl.ds(first + k, 1), :] = out[pl.ds(first + k, 1), :] + guess
            for r in range(ROWS):
                at = pl.ds(first + HEAVY + rows[r], 1)
                out[at, :] = out[at, :] - signs[r] * guess
    for j in range(2):
        at = pl.ds(mine + j * OUT_ROWS + HEAVY, SKETCH)
        out[at, :] = out[at, :] + err[j * SKETCH : (j + 1) * SKETCH, :]


def local_part(activations, cotangent, error_sketch, buckets, sign_bits, heavy_blocks, where):
    bkt, sgn = buckets.transpose(2, 0, 1), sign_bits.transpose(2, 0, 1)
    error = error_sketch.reshape(SKETCH, 2, BLK).transpose(1, 0, 2).reshape(2 * SKETCH, BLK)
    vmem = pl.BlockSpec(memory_space=pltpu.VMEM)
    smem = pl.BlockSpec(memory_space=pltpu.SMEM)
    return pl.pallas_call(
        kernel,
        out_shape=jax.ShapeDtypeStruct((BLK * OUT_ROWS, BLK), F32),
        in_specs=[vmem] * 5 + [smem] * 4,
        out_specs=vmem,
        scratch_shapes=[
            pltpu.VMEM((TOK * ROW_BLOCKS, BLK), F32),
            pltpu.VMEM((DEPTH, BLK), F32),
            pltpu.VMEM((SKETCH * KC, KIN), BF16),
            pltpu.VMEM((DEPTH, SKETCH * BLK), BF16),
            pltpu.VMEM((DEPTH, SKETCH * BLK), BF16),
            pltpu.VMEM((HEAVY, BLK, BLK), F32),
        ],
        compiler_params=pltpu.CompilerParams(vmem_limit_bytes=48 * 1024 * 1024),
        name="sketch_block",
    )(activations, cotangent, bkt, sgn, error, heavy_blocks, bkt, sgn, where)


def body(activations, cotangent, error_sketch, buckets, sign_bits, heavy_blocks):
    where = lax.axis_index("dp").astype(jnp.int32).reshape(1)
    local = local_part(activations, cotangent, error_sketch, buckets, sign_bits, heavy_blocks, where)
    part = lax.all_to_all(local.reshape(4, 32 * OUT_ROWS, BLK), "dp", 0, 0, axis_index_groups=NEAR).sum(axis=0)
    part = lax.all_to_all(part.reshape(16, 2 * OUT_ROWS, BLK), "dp", 0, 0, axis_index_groups=FAR).sum(axis=0)
    total = part.reshape(2, OUT_ROWS, BLK).transpose(1, 0, 2).reshape(3, 8, 2 * BLK)
    return total[:1], total[1:][None]


def solution(mesh):
    return jax.shard_map(
        body,
        mesh=mesh,
        in_specs=(
            P("dp", None),
            P("dp", "mp"),
            P("mp", None, None, "dp"),
            P(None, None, "mp"),
            P(None, None, "mp"),
            P("mp"),
        ),
        out_specs=(P("mp", None, "dp"), P("mp", None, None, "dp")),
        check_vma=False,
    )
```

time: 331 us -> 71.1 us (0.21)
  waiting for transfers between devices: 164 us -> 0 us
  matrix products: 88.8 us -> 0 us
  local copies, waits for them, and re-layouts: 61.4 us -> 6.43 us
  blocking collectives: 0 us -> 53.2 us
  between operations: 14.2 us -> 0.66 us
  Pallas kernels: 0 us -> 10.2 us
    psum x1 -> x0, waiting for transfers between devices: 164 us -> none  [body(): summed = lax.psum(local, 'dp')]
    dot_general x13 -> x0, matrix products: 88.8 us -> none  [the longest x5 43.9 us: add_group(): jnp.einsum('rbac,tcq->tarbq', map_part, cot_blocks, precision=high)]
    all_to_all x0 -> x2, blocking collectives: none -> 53.2 us  [the longest x1 29 us: body(): lax.all_to_all(part.reshape(16, 2 * OUT_ROWS, BLK), 'dp', 0, 0, axis_inde...]
    transpose x5 -> x0, local copies, waits for them, and re-layouts: 43.3 us -> none  [add_group(): jnp.einsum('rbac,tcq->tarbq', map_part, cot_blocks, precision=high)]
    pallas_call x0 -> x1, Pallas kernels: none -> 10.2 us  [local_part(): pl.pallas_call(kernel, out_shape=jax.ShapeDtypeStruct((BLK * OUT_ROWS, BL...]
    dynamic_slice x5 -> x0, local copies, waits for them, and re-layouts: 4.86 us -> none  [add_group(): lax.dynamic_slice_in_dim(activations, index * group, group, 1)]
    gather x4 -> x0, local copies, waits for them, and re-layouts: 3.36 us -> none  [the longest x1 1.65 us: body(): jnp.take(cotangent.reshape(tok_rows, col_blocks, block), heavy_col, axis=1)]
  transfers between devices with their start and end apart: 1 -> 0, of which waited for: 1 -> 0; matrix products, arithmetic and copies ran while one was open for 1% -> 0% of each run, Pallas kernels for 0% -> 0%
where the time goes in v1:
time: 71.1 us; the launch traced here: 70.6 us
  blocking collectives  53.2 us (75%)
  Pallas kernels  10.2 us (14%)
  local copies, waits for them, and re-layouts  6.43 us (9%)
    all_to_all x1, blocking collectives, body(): lax.all_to_all(part.reshape(16, 2 * OUT_ROWS, BLK), 'dp', 0, 0, axis_inde...  29 us
    all_to_all x1, blocking collectives, body(): lax.all_to_all(local.reshape(4, 32 * OUT_ROWS, BLK), 'dp', 0, 0, axis_ind...  24.2 us
    pallas_call x1, Pallas kernels, local_part(): pl.pallas_call(kernel, out_shape=jax.ShapeDtypeStruct((BLK * OUT_ROWS, BL...  10.2 us
    unnamed x10, local copies, waits for them, and re-layouts  4.46 us

profile of v1, /device:TPU:6, one launch (start us, length us, event | category | flops | bytes accessed | tf_op | source)
XLA Modules:
  0.0 70.6 jit_solution(7328073199459622988)
XLA Ops:
  0.6 0.7 %reshape.26 = f32[16,2,128]{2,1,0:T(2,128)S(1)} reshape(f32[1,2,8,256]{3,2,1,0:T(8,128)} %param.8) | data formatting | bytes 32768 | tf_op jit(solution)/shard_map/reshape | solution.py:141
  1.4 0.0 copy-start
  1.4 1.3 %copy-done = bf16[128,5120]{1,0:T(8,128)(2,1)S(1)} copy-done((bf16[128,5120]{1,0:T(8,128)(2,1)S(1)}, bf16[128,5120]{1,0:T(8,128)(2,1)}, u32[]{:S(2)}) %copy-start) | copy-done | bytes 1310744
  2.7 0.0 copy-start.1
  2.7 1.1 %copy-done.1 = bf16[128,2176]{1,0:T(8,128)(2,1)S(1)} copy-done((bf16[128,2176]{1,0:T(8,128)(2,1)S(1)}, bf16[128,2176]{1,0:T(8,128)(2,1)}, u32[]{:S(2)}) %copy-start.1) | copy-done | bytes 557080
  3.7 0.0 copy-start.2
  3.8 0.7 %copy-done.2 = s32[2,40,17]{1,0,2:T(2,128)S(1)} copy-done((s32[2,40,17]{1,0,2:T(2,128)S(1)}, s32[2,40,17]{1,0,2:T(2,128)}, u32[]{:S(2)}) %copy-start.2) | copy-done | bytes 5464
  4.5 0.0 copy-start.3
  4.5 0.7 %copy-done.3 = s32[2,40,17]{1,0,2:T(2,128)S(1)} copy-done((s32[2,40,17]{1,0,2:T(2,128)S(1)}, s32[2,40,17]{1,0,2:T(2,128)}, u32[]{:S(2)}) %copy-start.3) | copy-done | bytes 5464
  5.2 0.0 copy-start.4
  5.2 0.7 copy-done.4
  5.8 10.2 %sketch_block.1 = f32[3072,128]{1,0:T(8,128)S(1)} custom-call(bf16[128,5120]{1,0:T(8,128)(2,1)S(1)} %copy-done, bf16[128,2176]{1,0:T(8,128)(2,1)S(1)} %copy-done.1, s32[17,2,40]{2,1,0:T(2,128)S(1)} %bitcast.16, s32[17,2,40]{2,1,0:T(2,128)S(1)} %bitcast.18, f32[32,128]{1,0:T(8,128)S(1)} %bitcast.20, s32[8]{0:T(128)S(1)} %copy-done.4, ...), custom_call_target="tpu_custom_call" | custom-call | tf_op jit(solution)/shard_map/sketch_block/pallas_call | solution.py:144
  16.0 24.2 %all_to_all.10 = f32[4,768,128]{2,1,0:T(8,128)S(1)} all-to-all(f32[4,768,128]{2,1,0:T(8,128)S(1)} %bitcast.15), channel_id=1, replica_groups={{0,8,64,72},{16,24,80,88},{32,40,96,104},{48,56,112,120},{128,136,192,2..., dimensions={0} | all-to-all | bytes 3145728 | tf_op jit(solution)/shard_map/all_to_all | solution.py:165
  40.2 0.1 reduce_sum.18
  40.4 29.0 %all_to_all.11 = f32[16,48,128]{2,1,0:T(8,128)S(1)} all-to-all(f32[16,48,128]{2,1,0:T(8,128)S(1)} %bitcast.21), channel_id=1, replica_groups={{0,16,32,48,128,144,160,176,256,272,288,304,384,400,416,432},{8,24,40,5..., dimensions={0} | all-to-all | bytes 786432 | tf_op jit(solution)/shard_map/all_to_all | solution.py:166
  69.3 0.6 slice_bitcast_fusion
  70.0 0.6 broadcast_in_dim.3
  (4 shorter events, 0.0 us)
Async XLA Ops:
  1.4 1.3 %copy-start = (bf16[128,5120]{1,0:T(8,128)(2,1)S(1)}, bf16[128,5120]{1,0:T(8,128)(2,1)}, u32[]{:S(2)}) copy-start(bf16[128,5120]{1,0:T(8,128)(2,1)} %act.1) | copy-start | bytes 3932164
  2.7 1.1 %copy-start.1 = (bf16[128,2176]{1,0:T(8,128)(2,1)S(1)}, bf16[128,2176]{1,0:T(8,128)(2,1)}, u32[]{:S(2)}) copy-start(bf16[128,2176]{1,0:T(8,128)(2,1)} %cot.1) | copy-start | bytes 1671172
  3.7 0.7 %copy-start.2 = (s32[2,40,17]{1,0,2:T(2,128)S(1)}, s32[2,40,17]{1,0,2:T(2,128)}, u32[]{:S(2)}) copy-start(s32[2,40,17]{1,0,2:T(2,128)} %param.9) | copy-start | bytes 16324
  4.5 0.7 %copy-start.3 = (s32[2,40,17]{1,0,2:T(2,128)S(1)}, s32[2,40,17]{1,0,2:T(2,128)}, u32[]{:S(2)}) copy-start(s32[2,40,17]{1,0,2:T(2,128)} %param.10) | copy-start | bytes 16324
  5.2 0.7 copy-start.4

commit v2 on v1

v2 whole, which is shorter than its diff:
```python
import functools
import jax
import jax.numpy as jnp
from jax import lax
from jax.experimental import pallas as pl
from jax.experimental.pallas import tpu as pltpu
from jax.sharding import PartitionSpec as P

ROWS = 2
BUCKETS = 8
HEAVY = 8
BLK = 128
TOK = 128
ROW_BLOCKS = 40
COL_BLOCKS = 17
CPAD = 18
GRP = 4
GROUPS = TOK // GRP
KIN = GRP * ROW_BLOCKS
KC = GRP * CPAD
SKETCH = ROWS * BUCKETS
OUT_ROWS = HEAVY + SKETCH
DEPTH = GROUPS * KC
TN = (((0,), (0,)), ((), ()))
F32 = jnp.float32
BF16 = jnp.bfloat16
PAIR = 4
BLOCKS = GROUPS // 2
CUTS = 1
SIDE = 8
NEAR = [[(2 * a + i) * SIDE + 2 * b + j for i in range(2) for j in range(2)] for a in range(4) for b in range(4)]
FAR = [[(2 * a + i) * SIDE + 2 * b + j for a in range(4) for b in range(4)] for i in range(2) for j in range(2)]


def iota(shape, dim):
    return lax.broadcasted_iota(jnp.int32, shape, dim)


def place(p):
    dp = p // 2
    y, z = dp // SIDE, dp % SIDE
    return (((y % 2) * 2 + z % 2) * 16 + (y // 2) * 4 + z // 2) * 2 + p % 2


def kernel(
    act_h, cot_h, err_h, bkt_h, sgn_h, heavy_h, where,
    out,
    act, cot, err4, bkt, sgn, heavy, bkt_s, sgn_s, err, act3, cot3, maps, actb, lhs, hi_a, lo_a, hi_b, lo_b, sems,
):
    pairs = [
        (bkt_h, bkt), (sgn_h, sgn), (act_h, act), (cot_h, cot),
        (heavy_h, heavy), (bkt_h, bkt_s), (sgn_h, sgn_s), (err_h, err4),
    ]
    copies = [pltpu.make_async_copy(a, b, sems.at[i]) for i, (a, b) in enumerate(pairs)]
    for copy in copies:
        copy.start()
    perm = (place(iota((BLK, BLK), 0)) == iota((BLK, BLK), 1)).astype(BF16)
    spread_rows = (iota((KC, COL_BLOCKS), 0) % CPAD == iota((KC, COL_BLOCKS), 1)).astype(F32)
    spread_cols = (iota((ROW_BLOCKS, KIN), 1) % ROW_BLOCKS == iota((ROW_BLOCKS, KIN), 0)).astype(F32)
    own = (iota((KC, KIN), 0) // CPAD == iota((KC, KIN), 1) // ROW_BLOCKS) & (
        iota((KC, KIN), 0) % CPAD < COL_BLOCKS
    )
    copies[0].wait()
    copies[1].wait()
    copies[4].wait()
    times = jnp.ones((COL_BLOCKS, ROW_BLOCKS), F32)
    for k in range(HEAVY):
        a, c = lax.div(heavy[k], COL_BLOCKS), lax.rem(heavy[k], COL_BLOCKS)
        here = (iota(times.shape, 0) == c) & (iota(times.shape, 1) == a)
        times = times - here.astype(F32)

    def spread(x):
        return jnp.dot(jnp.dot(spread_rows, x, preferred_element_type=F32), spread_cols, preferred_element_type=F32)

    for r in range(ROWS):
        weight = spread((2 * sgn[:, r, :] - 1).astype(F32) * times)
        bucket = jnp.where(own, spread(bkt[:, r, :].astype(F32)), -1.0)
        for b in range(0, BUCKETS, 2):
            two = [jnp.where(bucket == bb, weight, 0.0) for bb in (b, b + 1)]
            at = (r * BUCKETS + b) * KC
            maps[at : at + 2 * KC, :] = jnp.concatenate(two, axis=0).astype(BF16)

    copies[2].wait()
    for a in range(ROW_BLOCKS):
        act3[pl.ds(a, TOK, stride=ROW_BLOCKS), :] = jnp.dot(
            act[:, a * BLK : (a + 1) * BLK], perm, preferred_element_type=F32
        )
    copies[3].wait()
    for c in range(COL_BLOCKS):
        cot3[pl.ds(c, TOK, stride=CPAD), :] = cot[:, c * BLK : (c + 1) * BLK].astype(F32)
    cot3[pl.ds(COL_BLOCKS, TOK, stride=CPAD), :] = jnp.zeros((TOK, BLK), F32)

    inverse = 1.0 / TOK
    for copy in copies[5:]:
        copy.wait()
    for r in range(ROWS):
        for j in range(2):
            err[j * SKETCH + r * BUCKETS : j * SKETCH + (r + 1) * BUCKETS, :] = err4[0, r, :, j * BLK : (j + 1) * BLK]
    for k in range(HEAVY):
        a = lax.div(heavy[k], COL_BLOCKS)
        c = lax.rem(heavy[k], COL_BLOCKS)
        block = lax.dot_general(
            act3[pl.ds(a, TOK, stride=ROW_BLOCKS), :].astype(BF16),
            cot[:, pl.ds(pl.multiple_of(c * BLK, BLK), BLK)],
            TN,
            preferred_element_type=F32,
        ) * inverse
        out[pl.ds(k, BLK, stride=OUT_ROWS), :] = block

    for i in range(BLOCKS):
        for h in range(2):
            actb[i, :, h * BLK : (h + 1) * BLK] = act3[(2 * i + h) * KIN : (2 * i + h + 1) * KIN, :].astype(BF16)
    lhs[...] = cot3[...].T.astype(BF16)

    def weigh(g, i, hi, lo):
        many = jnp.dot(maps[g * PAIR * KC : (g + 1) * PAIR * KC, :], actb[i], preferred_element_type=F32)
        rows = slice(i * 2 * KC, (i + 1) * 2 * KC)
        for j in range(PAIR):
            w = many[j * KC : (j + 1) * KC]
            w = jnp.concatenate([w[:, :BLK], w[:, BLK:]], axis=0)
            top = w.astype(BF16)
            hi[rows, j * BLK : (j + 1) * BLK] = top
            lo[rows, j * BLK : (j + 1) * BLK] = (w - top.astype(F32)).astype(BF16)

    def fold(g, hi, lo):
        for t in range(PAIR // 2):
            total = None
            for part in (hi, lo):
                for k in range(CUTS):
                    deep = slice(k * DEPTH // CUTS, (k + 1) * DEPTH // CUTS)
                    term = jnp.dot(
                        lhs[:, deep], part[deep, 2 * t * BLK : 2 * (t + 1) * BLK], preferred_element_type=F32
                    )
                    total = term if total is None else total + term
                    yield
            for j in range(2):
                at = HEAVY + g * PAIR + 2 * t + j
                out[pl.ds(at, BLK, stride=OUT_ROWS), :] = total[:, j * BLK : (j + 1) * BLK].T * inverse

    steps = SKETCH // PAIR
    slots = [(hi_a, lo_a), (hi_b, lo_b)]
    for i in range(BLOCKS):
        weigh(0, i, *slots[0])
    for g in range(steps):
        sums = fold(g, *slots[g % 2])
        count = PAIR * CUTS
        done = 0
        for i in range(BLOCKS):
            if g + 1 < steps:
                weigh(g + 1, i, *slots[(g + 1) % 2])
            while done * BLOCKS < (i + 1) * count:
                next(sums, None)
                done += 1
        for _ in sums:
            pass

    mine = place(2 * where[0]) * OUT_ROWS
    for k in range(HEAVY):
        a = lax.div(heavy[k], COL_BLOCKS)
        c = lax.rem(heavy[k], COL_BLOCKS)
        signs = [(2 * sgn_s[c, r, a] - 1).astype(F32) for r in range(ROWS)]
        rows = [r * BUCKETS + bkt_s[c, r, a] for r in range(ROWS)]
        for j in range(2):
            first = mine + j * OUT_ROWS
            guess = jnp.zeros((1, BLK), F32)
            for r in range(ROWS):
                guess = guess + signs[r] * err[pl.ds(j * SKETCH + rows[r], 1), :]
            guess = guess * (1.0 / ROWS)
            out[pl.ds(first + k, 1), :] = out[pl.ds(first + k, 1), :] + guess
            for r in range(ROWS):
                at = pl.ds(first + HEAVY + rows[r], 1)
                out[at, :] = out[at, :] - signs[r] * guess
    for j in range(2):
        at = pl.ds(mine + j * OUT_ROWS + HEAVY, SKETCH)
        out[at, :] = out[at, :] + err[j * SKETCH : (j + 1) * SKETCH, :]


def local_part(activations, cotangent, error_sketch, buckets, sign_bits, heavy_blocks, where):
    bkt, sgn = buckets.transpose(2, 0, 1), sign_bits.transpose(2, 0, 1)
    hbm = pl.BlockSpec(memory_space=pltpu.HBM)
    return pl.pallas_call(
        kernel,
        out_shape=jax.ShapeDtypeStruct((BLK * OUT_ROWS, BLK), F32),
        in_specs=[hbm] * 6 + [pl.BlockSpec(memory_space=pltpu.SMEM)],
        out_specs=pl.BlockSpec(memory_space=pltpu.VMEM),
        scratch_shapes=[
            pltpu.VMEM(activations.shape, BF16),
            pltpu.VMEM(cotangent.shape, BF16),
            pltpu.VMEM(error_sketch.shape, F32),
            pltpu.VMEM(bkt.shape, jnp.int32),
            pltpu.VMEM(sgn.shape, jnp.int32),
            pltpu.SMEM(heavy_blocks.shape, jnp.int32),
            pltpu.SMEM(bkt.shape, jnp.int32),
            pltpu.SMEM(sgn.shape, jnp.int32),
            pltpu.VMEM((2 * SKETCH, BLK), F32),
            pltpu.VMEM((TOK * ROW_BLOCKS, BLK), F32),
            pltpu.VMEM((DEPTH, BLK), F32),
            pltpu.VMEM((SKETCH * KC, KIN), BF16),
            pltpu.VMEM((BLOCKS, KIN, 2 * BLK), BF16),
            pltpu.VMEM((BLK, DEPTH), BF16),
            pltpu.VMEM((DEPTH, PAIR * BLK), BF16),
            pltpu.VMEM((DEPTH, PAIR * BLK), BF16),
            pltpu.VMEM((DEPTH, PAIR * BLK), BF16),
            pltpu.VMEM((DEPTH, PAIR * BLK), BF16),
            pltpu.SemaphoreType.DMA((8,)),
        ],
        compiler_params=pltpu.CompilerParams(vmem_limit_bytes=60 * 1024 * 1024),
        name="sketch_block",
    )(activations, cotangent, error_sketch, bkt, sgn, heavy_blocks, where)


def body(activations, cotangent, error_sketch, buckets, sign_bits, heavy_blocks):
    where = lax.axis_index("dp").astype(jnp.int32).reshape(1)
    local = local_part(activations, cotangent, error_sketch, buckets, sign_bits, heavy_blocks, where)
    part = lax.all_to_all(local.reshape(4, 32 * OUT_ROWS, BLK), "dp", 0, 0, axis_index_groups=NEAR).sum(axis=0)
    part = lax.all_to_all(part.reshape(16, 2 * OUT_ROWS, BLK), "dp", 0, 0, axis_index_groups=FAR).sum(axis=0)
    total = part.reshape(2, OUT_ROWS, BLK).transpose(1, 0, 2).reshape(3, 8, 2 * BLK)
    return total[:1], total[1:][None]


def solution(mesh):
    return jax.shard_map(
        body,
        mesh=mesh,
        in_specs=(
            P("dp", None),
            P("dp", "mp"),
            P("mp", None, None, "dp"),
            P(None, None, "mp"),
            P(None, None, "mp"),
            P("mp"),
        ),
        out_specs=(P("mp", None, "dp"), P("mp", None, None, "dp")),
        check_vma=False,
    )
```

time: 71.1 us -> 66.9 us (0.941)
  the two profiles are of different devices: /device:TPU:6 before, /device:TPU:11 now
where the time goes in v2:
time: 66.9 us; the launch traced here: 66.6 us
  blocking collectives  55.3 us (83%)
  Pallas kernels  9.3 us (14%)
  local copies, waits for them, and re-layouts  1.24 us (2%)
    all_to_all x1, blocking collectives, body(): lax.all_to_all(part.reshape(16, 2 * OUT_ROWS, BLK), 'dp', 0, 0, axis_inde...  32.7 us
    all_to_all x1, blocking collectives, body(): lax.all_to_all(local.reshape(4, 32 * OUT_ROWS, BLK), 'dp', 0, 0, axis_ind...  22.6 us
    pallas_call x1, Pallas kernels, local_part(): pl.pallas_call(kernel, out_shape=jax.ShapeDtypeStruct((BLK * OUT_ROWS, BL...  9.3 us

profile of v2, /device:TPU:11, one launch (start us, length us, event | category | flops | bytes accessed | tf_op | source)
XLA Modules:
  0.0 66.6 jit_solution(1294592153836217908)
XLA Ops:
  0.6 9.3 %sketch_block.1 = f32[3072,128]{1,0:T(8,128)} custom-call(bf16[128,5120]{1,0:T(8,128)(2,1)} %act_h.1, bf16[128,2176]{1,0:T(8,128)(2,1)} %cot_h.1, f32[1,2,8,256]{3,2,1,0:T(8,128)} %err_h.1, s32[17,2,40]{2,1,0:T(2,128)} %bitcast.14, s32[17,2,40]{2,1,0:T(2,128)} %bitcast.15, s32[8]{0:T(128)} %heavy_h.1, s32[1]{0:T(128)} %bitcast.2.where), custom_call_target="tpu_custom_call" | custom-call | tf_op jit(solution)/shard_map/sketch_block/pallas_call | solution.py:181
  9.9 22.6 %all_to_all.10 = f32[4,768,128]{2,1,0:T(8,128)S(1)} all-to-all(f32[4,768,128]{2,1,0:T(8,128)} %bitcast.10), channel_id=1, replica_groups={{0,8,64,72},{16,24,80,88},{32,40,96,104},{48,56,112,120},{128,136,192,2..., dimensions={0} | all-to-all | bytes 3145728 | tf_op jit(solution)/shard_map/all_to_all | solution.py:215
  32.5 0.1 reduce_sum.18
  32.6 32.7 %all_to_all.11 = f32[16,48,128]{2,1,0:T(8,128)S(1)} all-to-all(f32[16,48,128]{2,1,0:T(8,128)S(1)} %bitcast.11), channel_id=1, replica_groups={{0,16,32,48,128,144,160,176,256,272,288,304,384,400,416,432},{8,24,40,5..., dimensions={0} | all-to-all | bytes 786432 | tf_op jit(solution)/shard_map/all_to_all | solution.py:216
  65.4 0.6 slice_bitcast_fusion
  66.0 0.6 broadcast_in_dim.3
  (3 shorter events, 0.0 us)

commit v3 on v2

--- a/solution.py
+++ b/solution.py
@@ -28,7 +28,30 @@
 BLOCKS = GROUPS // 2
 CUTS = 1
 SIDE = 8
-NEAR = [[(2 * a + i) * SIDE + 2 * b + j for i in range(2) for j in range(2)] for a in range(4) for b in range(4)]
+MODEL = 8
+
+
+def mate(v, half):
+    return (v + 1 if (v + half) % 2 == 0 else v - 1) % SIDE
+
+
+def near_groups():
+    groups = set()
+    for m in range(MODEL):
+        for y in range(SIDE):
+            for z in range(SIDE):
+                ys, zs = {y, mate(y, m % 2)}, {z, mate(z, m % 2)}
+                groups.add(
+                    tuple(
+                        (u * SIDE + v) * MODEL + m
+                        for u in sorted(ys, key=lambda t: t % 2)
+                        for v in sorted(zs, key=lambda t: t % 2)
+                    )
+                )
+    return [list(g) for g in sorted(groups)]
+
+
+NEAR = near_groups()
 FAR = [[(2 * a + i) * SIDE + 2 * b + j for a in range(4) for b in range(4)] for i in range(2) for j in range(2)]
 
 
@@ -212,7 +235,7 @@
 def body(activations, cotangent, error_sketch, buckets, sign_bits, heavy_blocks):
     where = lax.axis_index("dp").astype(jnp.int32).reshape(1)
     local = local_part(activations, cotangent, error_sketch, buckets, sign_bits, heavy_blocks, where)
-    part = lax.all_to_all(local.reshape(4, 32 * OUT_ROWS, BLK), "dp", 0, 0, axis_index_groups=NEAR).sum(axis=0)
+    part = lax.all_to_all(local.reshape(4, 32 * OUT_ROWS, BLK), ("dp", "mp"), 0, 0, axis_index_groups=NEAR).sum(axis=0)
     part = lax.all_to_all(part.reshape(16, 2 * OUT_ROWS, BLK), "dp", 0, 0, axis_index_groups=FAR).sum(axis=0)
     total = part.reshape(2, OUT_ROWS, BLK).transpose(1, 0, 2).reshape(3, 8, 2 * BLK)
     return total[:1], total[1:][None]

time: 66.9 us -> 62.4 us (0.933)
  the two profiles are of different devices: /device:TPU:11 before, /device:TPU:6 now
where the time goes in v3:
time: 62.4 us; the launch traced here: 61.4 us
  blocking collectives  50 us (80%)
  Pallas kernels  9.3 us (15%)
  local copies, waits for them, and re-layouts  1.24 us (2%)
  between operations  0.65 us (1%)
    all_to_all x1, blocking collectives, body(): lax.all_to_all(part.reshape(16, 2 * OUT_ROWS, BLK), 'dp', 0, 0, axis_inde...  32.6 us
    all_to_all x1, blocking collectives, body(): lax.all_to_all(local.reshape(4, 32 * OUT_ROWS, BLK), ('dp', 'mp'), 0, 0,...  17.4 us
    pallas_call x1, Pallas kernels, local_part(): pl.pallas_call(kernel, out_shape=jax.ShapeDtypeStruct((BLK * OUT_ROWS, BL...  9.3 us

profile of v3, /device:TPU:6, one launch (start us, length us, event | category | flops | bytes accessed | tf_op | source)
XLA Modules:
  0.0 61.4 jit_solution(13568854307728462768)
XLA Ops:
  0.6 9.3 %sketch_block.1 = f32[3072,128]{1,0:T(8,128)} custom-call(bf16[128,5120]{1,0:T(8,128)(2,1)} %act_h.1, bf16[128,2176]{1,0:T(8,128)(2,1)} %cot_h.1, f32[1,2,8,256]{3,2,1,0:T(8,128)} %err_h.1, s32[17,2,40]{2,1,0:T(2,128)} %bitcast.14, s32[17,2,40]{2,1,0:T(2,128)} %bitcast.15, s32[8]{0:T(128)} %heavy_h.1, s32[1]{0:T(128)} %bitcast.2.where), custom_call_target="tpu_custom_call" | custom-call | tf_op jit(solution)/shard_map/sketch_block/pallas_call | solution.py:204
  9.9 17.4 %all_to_all.10 = f32[4,768,128]{2,1,0:T(8,128)S(1)} all-to-all(f32[4,768,128]{2,1,0:T(8,128)} %bitcast.10), channel_id=1, replica_groups={{0,8,64,72},{1,57,449,505},{2,10,66,74},{3,59,451,507},{4,12,68,76},{5,..., dimensions={0} | all-to-all | bytes 3145728 | tf_op jit(solution)/shard_map/all_to_all | solution.py:238
  27.3 0.1 reduce_sum.18
  27.5 32.6 %all_to_all.11 = f32[16,48,128]{2,1,0:T(8,128)S(1)} all-to-all(f32[16,48,128]{2,1,0:T(8,128)S(1)} %bitcast.11), channel_id=1, replica_groups={{0,16,32,48,128,144,160,176,256,272,288,304,384,400,416,432},{8,24,40,5..., dimensions={0} | all-to-all | bytes 786432 | tf_op jit(solution)/shard_map/all_to_all | solution.py:239
  60.1 0.6 slice_bitcast_fusion
  60.7 0.6 %broadcast_in_dim.3 = f32[1,2,8,256]{3,2,1,0:T(8,128)} reshape(f32[16,2,128]{2,1,0:T(2,128)S(1)} %copy.9) | data formatting | bytes 32768 | tf_op jit(solution)/shard_map/broadcast_in_dim | solution.py:241
  (3 shorter events, 0.0 us)

commit v4 on v2

--- a/solution.py
+++ b/solution.py
@@ -28,7 +28,24 @@
 BLOCKS = GROUPS // 2
 CUTS = 1
 SIDE = 8
-NEAR = [[(2 * a + i) * SIDE + 2 * b + j for i in range(2) for j in range(2)] for a in range(4) for b in range(4)]
+MODEL = 8
+
+
+def mate(v, half):
+    return (v + 1 if (v + half) % 2 == 0 else v - 1) % SIDE
+
+
+def near_pairs(step):
+    pairs = []
+    for y in range(SIDE):
+        for z in range(SIDE):
+            for m in range(MODEL):
+                u = mate(y, m % 2) if step & 2 else y
+                v = mate(z, m % 2) if step & 1 else z
+                pairs.append(((y * SIDE + z) * MODEL + m, (u * SIDE + v) * MODEL + m))
+    return pairs
+
+
 FAR = [[(2 * a + i) * SIDE + 2 * b + j for a in range(4) for b in range(4)] for i in range(2) for j in range(2)]
 
 
@@ -44,8 +61,8 @@
 
 def kernel(
     act_h, cot_h, err_h, bkt_h, sgn_h, heavy_h, where,
-    out,
-    act, cot, err4, bkt, sgn, heavy, bkt_s, sgn_s, err, act3, cot3, maps, actb, lhs, hi_a, lo_a, hi_b, lo_b, sems,
+    out_0, out_1, out_2, out_3,
+    act, cot, err4, bkt, sgn, heavy, bkt_s, sgn_s, err, act3, cot3, maps, actb, lhs, hi_a, lo_a, hi_b, lo_b, out, sems, out_sems,
 ):
     pairs = [
         (bkt_h, bkt), (sgn_h, sgn), (act_h, act), (cot_h, cot),
@@ -174,15 +191,26 @@
         at = pl.ds(mine + j * OUT_ROWS + HEAVY, SKETCH)
         out[at, :] = out[at, :] + err[j * SKETCH : (j + 1) * SKETCH, :]
 
+    quarter = BLK // 4 * OUT_ROWS
+    own_class = (where[0] // SIDE % 2) * 2 + where[0] % 2
+    sends = []
+    for step, part in enumerate((out_0, out_1, out_2, out_3)):
+        first = pl.multiple_of((own_class ^ step) * quarter, quarter)
+        sends.append(pltpu.make_async_copy(out.at[pl.ds(first, quarter), :], part, out_sems.at[step]))
+    for send in sends:
+        send.start()
+    for send in sends:
+        send.wait()
+
 
 def local_part(activations, cotangent, error_sketch, buckets, sign_bits, heavy_blocks, where):
     bkt, sgn = buckets.transpose(2, 0, 1), sign_bits.transpose(2, 0, 1)
     hbm = pl.BlockSpec(memory_space=pltpu.HBM)
     return pl.pallas_call(
         kernel,
-        out_shape=jax.ShapeDtypeStruct((BLK * OUT_ROWS, BLK), F32),
+        out_shape=[jax.ShapeDtypeStruct((BLK // 4 * OUT_ROWS, BLK), F32)] * 4,
         in_specs=[hbm] * 6 + [pl.BlockSpec(memory_space=pltpu.SMEM)],
-        out_specs=pl.BlockSpec(memory_space=pltpu.VMEM),
+        out_specs=[hbm] * 4,
         scratch_shapes=[
             pltpu.VMEM(activations.shape, BF16),
             pltpu.VMEM(cotangent.shape, BF16),
@@ -202,20 +230,47 @@
             pltpu.VMEM((DEPTH, PAIR * BLK), BF16),
             pltpu.VMEM((DEPTH, PAIR * BLK), BF16),
             pltpu.VMEM((DEPTH, PAIR * BLK), BF16),
+            pltpu.VMEM((BLK * OUT_ROWS, BLK), F32),
             pltpu.SemaphoreType.DMA((8,)),
+            pltpu.SemaphoreType.DMA((4,)),
         ],
         compiler_params=pltpu.CompilerParams(vmem_limit_bytes=60 * 1024 * 1024),
         name="sketch_block",
     )(activations, cotangent, error_sketch, bkt, sgn, heavy_blocks, where)
 
 
+def finish(parts, update, new_error):
+    total = jnp.sum(parts[...], axis=0)
+    for j in range(2):
+        cols = slice(j * BLK, (j + 1) * BLK)
+        row = j * OUT_ROWS
+        update[0, :, cols] = total[row : row + HEAVY]
+        for r in range(ROWS):
+            first = row + HEAVY + r * BUCKETS
+            new_error[0, r, :, cols] = total[first : first + BUCKETS]
+
+
+def outputs(parts):
+    vmem = pl.BlockSpec(memory_space=pltpu.VMEM)
+    return pl.pallas_call(
+        finish,
+        out_shape=(
+            jax.ShapeDtypeStruct((1, HEAVY, 2 * BLK), F32),
+            jax.ShapeDtypeStruct((1, ROWS, BUCKETS, 2 * BLK), F32),
+        ),
+        in_specs=[vmem],
+        out_specs=(vmem, vmem),
+        name="outputs",
+    )(parts)
+
+
 def body(activations, cotangent, error_sketch, buckets, sign_bits, heavy_blocks):
     where = lax.axis_index("dp").astype(jnp.int32).reshape(1)
-    local = local_part(activations, cotangent, error_sketch, buckets, sign_bits, heavy_blocks, where)
-    part = lax.all_to_all(local.reshape(4, 32 * OUT_ROWS, BLK), "dp", 0, 0, axis_index_groups=NEAR).sum(axis=0)
-    part = lax.all_to_all(part.reshape(16, 2 * OUT_ROWS, BLK), "dp", 0, 0, axis_index_groups=FAR).sum(axis=0)
-    total = part.reshape(2, OUT_ROWS, BLK).transpose(1, 0, 2).reshape(3, 8, 2 * BLK)
-    return total[:1], total[1:][None]
+    part, *others = local_part(activations, cotangent, error_sketch, buckets, sign_bits, heavy_blocks, where)
+    for step in (3, 2, 1):
+        part = part + lax.ppermute(others[step - 1], ("dp", "mp"), near_pairs(step))
+    parts = lax.all_to_all(part.reshape(16, 2 * OUT_ROWS, BLK), "dp", 0, 0, axis_index_groups=FAR)
+    return outputs(parts)
 
 
 def solution(mesh):

time: 66.9 us -> 62.7 us (0.937)
  the two profiles are of different devices: /device:TPU:11 before, /device:TPU:6 now
where the time goes in v4:
time: 62.7 us; the launch traced here: 62.1 us
  blocking collectives  31.9 us (51%)
  Pallas kernels  11 us (18%)
  starting transfers between devices  9.67 us (15%)
  waiting for transfers between devices  7.84 us (13%)
  other arithmetic  1.07 us (2%)
  between operations  0.67 us (1%)
    all_to_all x1, blocking collectives, body(): lax.all_to_all(part.reshape(16, 2 * OUT_ROWS, BLK), 'dp', 0, 0, axis_inde...  31.9 us
    ppermute x3, starting transfers between devices, body(): part = part + lax.ppermute(others[step - 1], ('dp', 'mp'), near_pairs(step))  9.67 us
    pallas_call x1, Pallas kernels, local_part(): pl.pallas_call(kernel, out_shape=[jax.ShapeDtypeStruct((BLK // 4 * OUT_RO...  9.35 us
    ppermute x3, waiting for transfers between devices, body(): part = part + lax.ppermute(others[step - 1], ('dp', 'mp'), near_pairs(step))  7.84 us
    pallas_call x1, Pallas kernels, outputs(): pl.pallas_call(finish, out_shape=(jax.ShapeDtypeStruct((1, HEAVY, 2 * BLK...  1.63 us
  transfers between devices with their start and end apart: 3, of which 3 were waited for; matrix products, arithmetic and copies ran while one was open for 0% of the time, Pallas kernels for 0%

profile of v4, /device:TPU:6, one launch (start us, length us, event | category | flops | bytes accessed | tf_op | source)
XLA Modules:
  0.0 62.1 jit_solution(772533168438704239)
XLA Ops:
  0.6 9.3 %sketch_block.1 = (f32[768,128]{1,0:T(8,128)}, f32[768,128]{1,0:T(8,128)}, f32[768,128]{1,0:T(8,128)}, f32[768,128]{1,0:T(8,128)}) custom-call(bf16[128,5120]{1,0:T(8,128)(2,1)} %act_h.1, bf16[128,2176]{1,0:T(8,128)(2,1)} %cot_h.1, f32[1,2,8,256]{3,2,1,0:T(8,128)} %err_h.1, s32[17,2,40]{2,1,0:T(2,128)} %bitcast.5, s32[17,2,40]{2,1,0:T(2,128)} %bitcast.6, ...), custom_call_target="tpu_custom_call" | custom-call | tf_op jit(solution)/shard_map/sketch_block/pallas_call | solution.py:209
  10.0 5.3 %collective-permute-start = (f32[768,128]{1,0:T(8,128)}, f32[768,128]{1,0:T(8,128)S(1)}, u32[]{:S(2)}, u32[]{:S(2)}) collective-permute-start(f32[768,128]{1,0:T(8,128)} %get-tuple-element.7), channel_id=1, source_target_pairs={{0,72},{1,505},{2,74},{3,507},{4,76},{5,509},{6,78},{7,511},{8,64}... | collective-permute-start | bytes 1179656 | tf_op jit(solution)/shard_map/ppermute | solution.py:271
  15.3 2.4 %collective-permute-start.1 = (f32[768,128]{1,0:T(8,128)}, f32[768,128]{1,0:T(8,128)S(1)}, u32[]{:S(2)}, u32[]{:S(2)}) collective-permute-start(f32[768,128]{1,0:T(8,128)} %get-tuple-element.8), channel_id=1, source_target_pairs={{0,64},{1,449},{2,66},{3,451},{4,68},{5,453},{6,70},{7,455},{8,72}... | collective-permute-start | bytes 1179656 | tf_op jit(solution)/shard_map/ppermute | solution.py:271
  17.6 2.0 %collective-permute-start.2 = (f32[768,128]{1,0:T(8,128)}, f32[768,128]{1,0:T(8,128)S(1)}, u32[]{:S(2)}, u32[]{:S(2)}) collective-permute-start(f32[768,128]{1,0:T(8,128)} %get-tuple-element.9), channel_id=1, source_target_pairs={{0,8},{1,57},{2,10},{3,59},{4,12},{5,61},{6,14},{7,63},{8,0},{9,17... | collective-permute-start | bytes 1179656 | tf_op jit(solution)/shard_map/ppermute | solution.py:271
  19.7 1.5 %collective-permute-done = f32[768,128]{1,0:T(8,128)S(1)} collective-permute-done((f32[768,128]{1,0:T(8,128)}, f32[768,128]{1,0:T(8,128)S(1)}, u32[]{:S(2)}, u32[]{:S(2)}) %collective-permute-start) | collective-permute-done | bytes 393248 | tf_op jit(solution)/shard_map/ppermute | solution.py:271
  21.2 4.6 %collective-permute-done.1 = f32[768,128]{1,0:T(8,128)S(1)} collective-permute-done((f32[768,128]{1,0:T(8,128)}, f32[768,128]{1,0:T(8,128)S(1)}, u32[]{:S(2)}, u32[]{:S(2)}) %collective-permute-start.1) | collective-permute-done | bytes 393248 | tf_op jit(solution)/shard_map/ppermute | solution.py:271
  25.9 1.6 %collective-permute-done.2 = f32[768,128]{1,0:T(8,128)S(1)} collective-permute-done((f32[768,128]{1,0:T(8,128)}, f32[768,128]{1,0:T(8,128)S(1)}, u32[]{:S(2)}, u32[]{:S(2)}) %collective-permute-start.2) | collective-permute-done | bytes 393248 | tf_op jit(solution)/shard_map/ppermute | solution.py:271
  27.5 1.1 %add_add_fusion = f32[768,128]{1,0:T(8,128)S(1)} fusion(f32[768,128]{1,0:T(8,128)S(1)} %collective-permute-done.2, f32[768,128]{1,0:T(8,128)S(1)} %collective-permute-done.1, f32[768,128]{1,0:T(8,128)} %get-tuple-element.6, f32[768,128]{1,0:T(8,128)S(1)} %collective-permute-done), kind=kLoop, calls=%fused_computation | loop fusion | flops 294912 | bytes 1966080 | tf_op jit(solution)/shard_map/add | solution.py:271
  28.6 31.9 %all_to_all.5.parts = f32[16,48,128]{2,1,0:T(8,128)} all-to-all(f32[16,48,128]{2,1,0:T(8,128)S(1)} %bitcast.4), channel_id=1, replica_groups={{0,16,32,48,128,144,160,176,256,272,288,304,384,400,416,432},{8,24,40,5..., dimensions={0} | all-to-all | bytes 786432 | tf_op jit(solution)/shard_map/all_to_all | solution.py:272
  60.5 1.6 %outputs.1 = (f32[1,8,256]{2,1,0:T(8,128)}, f32[1,2,8,256]{3,2,1,0:T(8,128)}) custom-call(f32[16,48,128]{2,1,0:T(8,128)} %all_to_all.5.parts), custom_call_target="tpu_custom_call" | custom-call | tf_op jit(solution)/shard_map/outputs/pallas_call | solution.py:255
Async XLA Ops:
  10.0 11.2 %collective-permute-start = (f32[768,128]{1,0:T(8,128)}, f32[768,128]{1,0:T(8,128)S(1)}, u32[]{:S(2)}, u32[]{:S(2)}) collective-permute-start(f32[768,128]{1,0:T(8,128)} %get-tuple-element.7), channel_id=1, source_target_pairs={{0,72},{1,505},{2,74},{3,507},{4,76},{5,509},{6,78},{7,511},{8,64}... | collective-permute-start | bytes 1179656 | tf_op jit(solution)/shard_map/ppermute | solution.py:271
  15.3 10.6 %collective-permute-start.1 = (f32[768,128]{1,0:T(8,128)}, f32[768,128]{1,0:T(8,128)S(1)}, u32[]{:S(2)}, u32[]{:S(2)}) collective-permute-start(f32[768,128]{1,0:T(8,128)} %get-tuple-element.8), channel_id=1, source_target_pairs={{0,64},{1,449},{2,66},{3,451},{4,68},{5,453},{6,70},{7,455},{8,72}... | collective-permute-start | bytes 1179656 | tf_op jit(solution)/shard_map/ppermute | solution.py:271
  17.6 9.9 %collective-permute-start.2 = (f32[768,128]{1,0:T(8,128)}, f32[768,128]{1,0:T(8,128)S(1)}, u32[]{:S(2)}, u32[]{:S(2)}) collective-permute-start(f32[768,128]{1,0:T(8,128)} %get-tuple-element.9), channel_id=1, source_target_pairs={{0,8},{1,57},{2,10},{3,59},{4,12},{5,61},{6,14},{7,63},{8,0},{9,17... | collective-permute-start | bytes 1179656 | tf_op jit(solution)/shard_map/ppermute | solution.py:271

commit v5 on v3

--- a/solution.py
+++ b/solution.py
@@ -59,16 +59,10 @@
     return lax.broadcasted_iota(jnp.int32, shape, dim)
 
 
-def place(p):
-    dp = p // 2
-    y, z = dp // SIDE, dp % SIDE
-    return (((y % 2) * 2 + z % 2) * 16 + (y // 2) * 4 + z // 2) * 2 + p % 2
-
-
 def kernel(
-    act_h, cot_h, err_h, bkt_h, sgn_h, heavy_h, where,
-    out,
-    act, cot, err4, bkt, sgn, heavy, bkt_s, sgn_s, err, act3, cot3, maps, actb, lhs, hi_a, lo_a, hi_b, lo_b, sems,
+    act_h, cot_h, err_h, bkt_h, sgn_h, heavy_h,
+    result,
+    act, cot, err4, bkt, sgn, heavy, bkt_s, sgn_s, err, extra, act3, cot3, maps, actb, lhs, hi_a, lo_a, hi_b, lo_b, out, sems, out_sems,
 ):
     pairs = [
         (bkt_h, bkt), (sgn_h, sgn), (act_h, act), (cot_h, cot),
@@ -77,7 +71,6 @@
     copies = [pltpu.make_async_copy(a, b, sems.at[i]) for i, (a, b) in enumerate(pairs)]
     for copy in copies:
         copy.start()
-    perm = (place(iota((BLK, BLK), 0)) == iota((BLK, BLK), 1)).astype(BF16)
     spread_rows = (iota((KC, COL_BLOCKS), 0) % CPAD == iota((KC, COL_BLOCKS), 1)).astype(F32)
     spread_cols = (iota((ROW_BLOCKS, KIN), 1) % ROW_BLOCKS == iota((ROW_BLOCKS, KIN), 0)).astype(F32)
     own = (iota((KC, KIN), 0) // CPAD == iota((KC, KIN), 1) // ROW_BLOCKS) & (
@@ -105,9 +98,7 @@
 
     copies[2].wait()
     for a in range(ROW_BLOCKS):
-        act3[pl.ds(a, TOK, stride=ROW_BLOCKS), :] = jnp.dot(
-            act[:, a * BLK : (a + 1) * BLK], perm, preferred_element_type=F32
-        )
+        act3[pl.ds(a, TOK, stride=ROW_BLOCKS), :] = act[:, a * BLK : (a + 1) * BLK].astype(F32)
     copies[3].wait()
     for c in range(COL_BLOCKS):
         cot3[pl.ds(c, TOK, stride=CPAD), :] = cot[:, c * BLK : (c + 1) * BLK].astype(F32)
@@ -130,6 +121,23 @@
         ) * inverse
         out[pl.ds(k, BLK, stride=OUT_ROWS), :] = block
 
+    for j in range(2):
+        old = err[j * SKETCH : (j + 1) * SKETCH, :]
+        guesses = jnp.zeros((HEAVY, BLK), F32)
+        for k in range(HEAVY):
+            a, c = lax.div(heavy[k], COL_BLOCKS), lax.rem(heavy[k], COL_BLOCKS)
+            signs = [(2 * sgn_s[c, r, a] - 1).astype(F32) for r in range(ROWS)]
+            rows = [r * BUCKETS + bkt_s[c, r, a] for r in range(ROWS)]
+            guess = jnp.zeros((1, BLK), F32)
+            for r in range(ROWS):
+                guess = guess + signs[r] * err[pl.ds(j * SKETCH + rows[r], 1), :]
+            guess = guess * (1.0 / ROWS)
+            guesses = jnp.where(iota((HEAVY, BLK), 0) == k, guess, guesses)
+            for r in range(ROWS):
+                old = old - jnp.where(iota((SKETCH, BLK), 0) == rows[r], signs[r] * guess, 0.0)
+        extra[j, :HEAVY, :] = guesses
+        extra[j, HEAVY:, :] = old
+
     for i in range(BLOCKS):
         for h in range(2):
             actb[i, :, h * BLK : (h + 1) * BLK] = act3[(2 * i + h) * KIN : (2 * i + h + 1) * KIN, :].astype(BF16)
@@ -177,35 +185,31 @@
         for _ in sums:
             pass
 
-    mine = place(2 * where[0]) * OUT_ROWS
-    for k in range(HEAVY):
-        a = lax.div(heavy[k], COL_BLOCKS)
-        c = lax.rem(heavy[k], COL_BLOCKS)
-        signs = [(2 * sgn_s[c, r, a] - 1).astype(F32) for r in range(ROWS)]
-        rows = [r * BUCKETS + bkt_s[c, r, a] for r in range(ROWS)]
-        for j in range(2):
-            first = mine + j * OUT_ROWS
-            guess = jnp.zeros((1, BLK), F32)
-            for r in range(ROWS):
-                guess = guess + signs[r] * err[pl.ds(j * SKETCH + rows[r], 1), :]
-            guess = guess * (1.0 / ROWS)
-            out[pl.ds(first + k, 1), :] = out[pl.ds(first + k, 1), :] + guess
-            for r in range(ROWS):
-                at = pl.ds(first + HEAVY + rows[r], 1)
-                out[at, :] = out[at, :] - signs[r] * guess
+    mine = lax.axis_index("dp") * (2 * OUT_ROWS)
     for j in range(2):
-        at = pl.ds(mine + j * OUT_ROWS + HEAVY, SKETCH)
-        out[at, :] = out[at, :] + err[j * SKETCH : (j + 1) * SKETCH, :]
-
-
-def local_part(activations, cotangent, error_sketch, buckets, sign_bits, heavy_blocks, where):
+        at = pl.ds(mine + j * OUT_ROWS, OUT_ROWS)
+        out[at, :] = out[at, :] + extra[j]
+
+    whole = out.reshape(SIDE // 2, 2, SIDE // 2, 2, 2 * OUT_ROWS, BLK)
+    sends = [
+        pltpu.make_async_copy(whole.at[:, i, :, j], result.at[2 * i + j], out_sems.at[2 * i + j])
+        for i in range(2)
+        for j in range(2)
+    ]
+    for send in sends:
+        send.start()
+    for send in sends:
+        send.wait()
+
+
+def local_part(activations, cotangent, error_sketch, buckets, sign_bits, heavy_blocks):
     bkt, sgn = buckets.transpose(2, 0, 1), sign_bits.transpose(2, 0, 1)
     hbm = pl.BlockSpec(memory_space=pltpu.HBM)
     return pl.pallas_call(
         kernel,
-        out_shape=jax.ShapeDtypeStruct((BLK * OUT_ROWS, BLK), F32),
-        in_specs=[hbm] * 6 + [pl.BlockSpec(memory_space=pltpu.SMEM)],
-        out_specs=pl.BlockSpec(memory_space=pltpu.VMEM),
+        out_shape=jax.ShapeDtypeStruct((4, SIDE // 2, SIDE // 2, 2 * OUT_ROWS, BLK), F32),
+        in_specs=[hbm] * 6,
+        out_specs=hbm,
         scratch_shapes=[
             pltpu.VMEM(activations.shape, BF16),
             pltpu.VMEM(cotangent.shape, BF16),
@@ -216,6 +220,7 @@
             pltpu.SMEM(bkt.shape, jnp.int32),
             pltpu.SMEM(sgn.shape, jnp.int32),
             pltpu.VMEM((2 * SKETCH, BLK), F32),
+            pltpu.VMEM((2, OUT_ROWS, BLK), F32),
             pltpu.VMEM((TOK * ROW_BLOCKS, BLK), F32),
             pltpu.VMEM((DEPTH, BLK), F32),
             pltpu.VMEM((SKETCH * KC, KIN), BF16),
@@ -225,20 +230,46 @@
             pltpu.VMEM((DEPTH, PAIR * BLK), BF16),
             pltpu.VMEM((DEPTH, PAIR * BLK), BF16),
             pltpu.VMEM((DEPTH, PAIR * BLK), BF16),
+            pltpu.VMEM((BLK * OUT_ROWS, BLK), F32),
             pltpu.SemaphoreType.DMA((8,)),
+            pltpu.SemaphoreType.DMA((4,)),
         ],
         compiler_params=pltpu.CompilerParams(vmem_limit_bytes=60 * 1024 * 1024),
         name="sketch_block",
-    )(activations, cotangent, error_sketch, bkt, sgn, heavy_blocks, where)
+    )(activations, cotangent, error_sketch, bkt, sgn, heavy_blocks)
+
+
+def finish(parts, update, new_error):
+    total = jnp.sum(parts[...], axis=0)
+    for j in range(2):
+        cols = slice(j * BLK, (j + 1) * BLK)
+        row = j * OUT_ROWS
+        update[0, :, cols] = total[row : row + HEAVY]
+        for r in range(ROWS):
+            first = row + HEAVY + r * BUCKETS
+            new_error[0, r, :, cols] = total[first : first + BUCKETS]
+
+
+def outputs(parts):
+    vmem = pl.BlockSpec(memory_space=pltpu.VMEM)
+    return pl.pallas_call(
+        finish,
+        out_shape=(
+            jax.ShapeDtypeStruct((1, HEAVY, 2 * BLK), F32),
+            jax.ShapeDtypeStruct((1, ROWS, BUCKETS, 2 * BLK), F32),
+        ),
+        in_specs=[vmem],
+        out_specs=(vmem, vmem),
+        compiler_params=pltpu.CompilerParams(vmem_limit_bytes=2 * 1024 * 1024),
+        name="outputs",
+    )(parts)
 
 
 def body(activations, cotangent, error_sketch, buckets, sign_bits, heavy_blocks):
-    where = lax.axis_index("dp").astype(jnp.int32).reshape(1)
-    local = local_part(activations, cotangent, error_sketch, buckets, sign_bits, heavy_blocks, where)
+    local = local_part(activations, cotangent, error_sketch, buckets, sign_bits, heavy_blocks)
     part = lax.all_to_all(local.reshape(4, 32 * OUT_ROWS, BLK), ("dp", "mp"), 0, 0, axis_index_groups=NEAR).sum(axis=0)
-    part = lax.all_to_all(part.reshape(16, 2 * OUT_ROWS, BLK), "dp", 0, 0, axis_index_groups=FAR).sum(axis=0)
-    total = part.reshape(2, OUT_ROWS, BLK).transpose(1, 0, 2).reshape(3, 8, 2 * BLK)
-    return total[:1], total[1:][None]
+    parts = lax.all_to_all(part.reshape(16, 2 * OUT_ROWS, BLK), "dp", 0, 0, axis_index_groups=FAR)
+    return outputs(parts)
 
 
 def solution(mesh):

time: 62.4 us -> 61.7 us (0.989)
  local copies, waits for them, and re-layouts: 1.24 us -> 0 us
    pallas_call x1 -> x2, Pallas kernels: 9.3 us -> 9.83 us  [the longest x1 9.19 us: local_part(): pl.pallas_call(kernel, out_shape=jax.ShapeDtypeStruct((4, SIDE // 2, SIDE...]
where the time goes in v5:
time: 61.7 us; the launch traced here: 60.7 us
  blocking collectives  50.1 us (81%)
  Pallas kernels  9.83 us (16%)
  between operations  0.64 us (1%)
    all_to_all x1, blocking collectives, body(): lax.all_to_all(part.reshape(16, 2 * OUT_ROWS, BLK), 'dp', 0, 0, axis_inde...  32.7 us
    all_to_all x1, blocking collectives, body(): lax.all_to_all(local.reshape(4, 32 * OUT_ROWS, BLK), ('dp', 'mp'), 0, 0,...  17.4 us
    pallas_call x1, Pallas kernels, local_part(): pl.pallas_call(kernel, out_shape=jax.ShapeDtypeStruct((4, SIDE // 2, SIDE...  9.19 us

profile of v5, /device:TPU:6, one launch (start us, length us, event | category | flops | bytes accessed | tf_op | source)
XLA Modules:
  0.0 60.7 jit_solution(18323033454510172994)
XLA Ops:
  0.6 9.2 %sketch_block.1 = f32[4,4,4,48,128]{4,3,2,1,0:T(8,128)} custom-call(bf16[128,5120]{1,0:T(8,128)(2,1)} %act_h.1, bf16[128,2176]{1,0:T(8,128)(2,1)} %cot_h.1, f32[1,2,8,256]{3,2,1,0:T(8,128)} %err_h.1, s32[17,2,40]{2,1,0:T(2,128)} %bitcast.6, s32[17,2,40]{2,1,0:T(2,128)} %bitcast.7, s32[8]{0:T(128)} %heavy_h.1), custom_call_target="tpu_custom_call" | custom-call | tf_op jit(solution)/shard_map/sketch_block/pallas_call | solution.py:208
  9.8 17.4 %all_to_all.10 = f32[4,768,128]{2,1,0:T(8,128)S(1)} all-to-all(f32[4,768,128]{2,1,0:T(8,128)} %bitcast.4), channel_id=1, replica_groups={{0,8,64,72},{1,57,449,505},{2,10,66,74},{3,59,451,507},{4,12,68,76},{5,..., dimensions={0} | all-to-all | bytes 3145728 | tf_op jit(solution)/shard_map/all_to_all | solution.py:270
  27.2 0.1 reduce_sum.9
  27.4 32.7 %all_to_all.11.parts = f32[16,48,128]{2,1,0:T(8,128)S(1)} all-to-all(f32[16,48,128]{2,1,0:T(8,128)S(1)} %bitcast.5), channel_id=1, replica_groups={{0,16,32,48,128,144,160,176,256,272,288,304,384,400,416,432},{8,24,40,5..., dimensions={0} | all-to-all | bytes 786432 | tf_op jit(solution)/shard_map/all_to_all | solution.py:271
  60.1 0.6 %outputs.1 = (f32[1,8,256]{2,1,0:T(8,128)}, f32[1,2,8,256]{3,2,1,0:T(8,128)}) custom-call(f32[16,48,128]{2,1,0:T(8,128)S(1)} %all_to_all.11.parts), custom_call_target="tpu_custom_call" | custom-call | tf_op jit(solution)/shard_map/outputs/pallas_call | solution.py:255

commit v6 on v5

--- a/solution.py
+++ b/solution.py
@@ -26,6 +26,8 @@
 BF16 = jnp.bfloat16
 PAIR = 4
 BLOCKS = GROUPS // 2
+PARTS = 4
+SHARE = TOK // PARTS
 CUTS = 1
 SIDE = 8
 MODEL = 8
@@ -65,9 +67,10 @@
     act, cot, err4, bkt, sgn, heavy, bkt_s, sgn_s, err, extra, act3, cot3, maps, actb, lhs, hi_a, lo_a, hi_b, lo_b, out, sems, out_sems,
 ):
     pairs = [
-        (bkt_h, bkt), (sgn_h, sgn), (act_h, act), (cot_h, cot),
+        (bkt_h, bkt), (sgn_h, sgn), (act_h.at[:SHARE], act.at[:SHARE]), (cot_h, cot),
         (heavy_h, heavy), (bkt_h, bkt_s), (sgn_h, sgn_s), (err_h, err4),
     ]
+    pairs += [(act_h.at[i * SHARE : (i + 1) * SHARE], act.at[i * SHARE : (i + 1) * SHARE]) for i in range(1, PARTS)]
     copies = [pltpu.make_async_copy(a, b, sems.at[i]) for i, (a, b) in enumerate(pairs)]
     for copy in copies:
         copy.start()
@@ -96,16 +99,25 @@
             at = (r * BUCKETS + b) * KC
             maps[at : at + 2 * KC, :] = jnp.concatenate(two, axis=0).astype(BF16)
 
-    copies[2].wait()
-    for a in range(ROW_BLOCKS):
-        act3[pl.ds(a, TOK, stride=ROW_BLOCKS), :] = act[:, a * BLK : (a + 1) * BLK].astype(F32)
+    def lay(part):
+        for a in range(ROW_BLOCKS):
+            act3[pl.ds(part * SHARE * ROW_BLOCKS + a, SHARE, stride=ROW_BLOCKS), :] = act[
+                part * SHARE : (part + 1) * SHARE, a * BLK : (a + 1) * BLK
+            ].astype(F32)
+        for i in range(part * BLOCKS // PARTS, (part + 1) * BLOCKS // PARTS):
+            for h in range(2):
+                actb[i, :, h * BLK : (h + 1) * BLK] = act3[(2 * i + h) * KIN : (2 * i + h + 1) * KIN, :].astype(BF16)
+
+    for i in range(PARTS):
+        copies[7 + i if i else 2].wait()
+        lay(i)
     copies[3].wait()
     for c in range(COL_BLOCKS):
         cot3[pl.ds(c, TOK, stride=CPAD), :] = cot[:, c * BLK : (c + 1) * BLK].astype(F32)
     cot3[pl.ds(COL_BLOCKS, TOK, stride=CPAD), :] = jnp.zeros((TOK, BLK), F32)
 
     inverse = 1.0 / TOK
-    for copy in copies[5:]:
+    for copy in copies[5:8]:
         copy.wait()
     for r in range(ROWS):
         for j in range(2):
@@ -138,9 +150,6 @@
         extra[j, :HEAVY, :] = guesses
         extra[j, HEAVY:, :] = old
 
-    for i in range(BLOCKS):
-        for h in range(2):
-            actb[i, :, h * BLK : (h + 1) * BLK] = act3[(2 * i + h) * KIN : (2 * i + h + 1) * KIN, :].astype(BF16)
     lhs[...] = cot3[...].T.astype(BF16)
 
     def weigh(g, i, hi, lo):
@@ -167,6 +176,23 @@
             for j in range(2):
                 at = HEAVY + g * PAIR + 2 * t + j
                 out[pl.ds(at, BLK, stride=OUT_ROWS), :] = total[:, j * BLK : (j + 1) * BLK].T * inverse
+
+    mine = lax.axis_index("dp") * (2 * OUT_ROWS)
+    whole = out.reshape(SIDE // 2, 2, SIDE // 2, 2, 2, OUT_ROWS, BLK)
+    sends = []
+
+    def send(first, count):
+        for j in range(2):
+            at = pl.ds(mine + j * OUT_ROWS + first, count)
+            out[at, :] = out[at, :] + extra[j, first : first + count, :]
+        for i in range(2):
+            for j in range(2):
+                rows = pl.ds(first, count)
+                copy = pltpu.make_async_copy(
+                    whole.at[:, i, :, j, :, rows], result.at[2 * i + j, :, :, :, rows], out_sems.at[len(sends)]
+                )
+                copy.start()
+                sends.append(copy)
 
     steps = SKETCH // PAIR
     slots = [(hi_a, lo_a), (hi_b, lo_b)]
@@ -184,22 +210,11 @@
                 done += 1
         for _ in sums:
             pass
-
-    mine = lax.axis_index("dp") * (2 * OUT_ROWS)
-    for j in range(2):
-        at = pl.ds(mine + j * OUT_ROWS, OUT_ROWS)
-        out[at, :] = out[at, :] + extra[j]
-
-    whole = out.reshape(SIDE // 2, 2, SIDE // 2, 2, 2 * OUT_ROWS, BLK)
-    sends = [
-        pltpu.make_async_copy(whole.at[:, i, :, j], result.at[2 * i + j], out_sems.at[2 * i + j])
-        for i in range(2)
-        for j in range(2)
-    ]
-    for send in sends:
-        send.start()
-    for send in sends:
-        send.wait()
+        if g == 1:
+            send(0, HEAVY + BUCKETS)
+    send(HEAVY + BUCKETS, BUCKETS)
+    for copy in sends:
+        copy.wait()
 
 
 def local_part(activations, cotangent, error_sketch, buckets, sign_bits, heavy_blocks):
@@ -207,7 +222,7 @@
     hbm = pl.BlockSpec(memory_space=pltpu.HBM)
     return pl.pallas_call(
         kernel,
-        out_shape=jax.ShapeDtypeStruct((4, SIDE // 2, SIDE // 2, 2 * OUT_ROWS, BLK), F32),
+        out_shape=jax.ShapeDtypeStruct((4, SIDE // 2, SIDE // 2, 2, OUT_ROWS, BLK), F32),
         in_specs=[hbm] * 6,
         out_specs=hbm,
         scratch_shapes=[
@@ -231,8 +246,8 @@
             pltpu.VMEM((DEPTH, PAIR * BLK), BF16),
             pltpu.VMEM((DEPTH, PAIR * BLK), BF16),
             pltpu.VMEM((BLK * OUT_ROWS, BLK), F32),
+            pltpu.SemaphoreType.DMA((7 + PARTS,)),
             pltpu.SemaphoreType.DMA((8,)),
-            pltpu.SemaphoreType.DMA((4,)),
         ],
         compiler_params=pltpu.CompilerParams(vmem_limit_bytes=60 * 1024 * 1024),
         name="sketch_block",

time: 61.7 us -> 61.2 us (level)
  no operation moved by 1% of the time
where the time goes in v6:
time: 61.2 us; the launch traced here: 60.2 us
  blocking collectives  50 us (82%)
  Pallas kernels  9.44 us (15%)
  between operations  0.64 us (1%)
    all_to_all x1, blocking collectives, body(): lax.all_to_all(part.reshape(16, 2 * OUT_ROWS, BLK), 'dp', 0, 0, axis_inde...  32.6 us
    all_to_all x1, blocking collectives, body(): lax.all_to_all(local.reshape(4, 32 * OUT_ROWS, BLK), ('dp', 'mp'), 0, 0,...  17.4 us
    pallas_call x1, Pallas kernels, local_part(): pl.pallas_call(kernel, out_shape=jax.ShapeDtypeStruct((4, SIDE // 2, SIDE...  8.81 us

profile of v6, /device:TPU:6, one launch (start us, length us, event | category | flops | bytes accessed | tf_op | source)
XLA Modules:
  0.0 60.2 jit_solution(6318497644840171090)
XLA Ops:
  0.6 8.8 %sketch_block.1 = f32[4,4,4,2,24,128]{5,4,3,2,1,0:T(8,128)} custom-call(bf16[128,5120]{1,0:T(8,128)(2,1)} %act_h.1, bf16[128,2176]{1,0:T(8,128)(2,1)} %cot_h.1, f32[1,2,8,256]{3,2,1,0:T(8,128)} %err_h.1, s32[17,2,40]{2,1,0:T(2,128)} %bitcast.6, s32[17,2,40]{2,1,0:T(2,128)} %bitcast.7, s32[8]{0:T(128)} %heavy_h.1), custom_call_target="tpu_custom_call" | custom-call | tf_op jit(solution)/shard_map/sketch_block/pallas_call | solution.py:223
  9.4 17.4 %all_to_all.10 = f32[4,768,128]{2,1,0:T(8,128)S(1)} all-to-all(f32[4,768,128]{2,1,0:T(8,128)} %bitcast.4), channel_id=1, replica_groups={{0,8,64,72},{1,57,449,505},{2,10,66,74},{3,59,451,507},{4,12,68,76},{5,..., dimensions={0} | all-to-all | bytes 3145728 | tf_op jit(solution)/shard_map/all_to_all | solution.py:285
  26.9 0.1 reduce_sum.9
  27.0 32.6 %all_to_all.11.parts = f32[16,48,128]{2,1,0:T(8,128)S(1)} all-to-all(f32[16,48,128]{2,1,0:T(8,128)S(1)} %bitcast.5), channel_id=1, replica_groups={{0,16,32,48,128,144,160,176,256,272,288,304,384,400,416,432},{8,24,40,5..., dimensions={0} | all-to-all | bytes 786432 | tf_op jit(solution)/shard_map/all_to_all | solution.py:286
  59.6 0.6 %outputs.1 = (f32[1,8,256]{2,1,0:T(8,128)}, f32[1,2,8,256]{3,2,1,0:T(8,128)}) custom-call(f32[16,48,128]{2,1,0:T(8,128)S(1)} %all_to_all.11.parts), custom_call_target="tpu_custom_call" | custom-call | tf_op jit(solution)/shard_map/outputs/pallas_call | solution.py:270

commit v7 on v5

--- a/solution.py
+++ b/solution.py
@@ -26,6 +26,8 @@
 BF16 = jnp.bfloat16
 PAIR = 4
 BLOCKS = GROUPS // 2
+PARTS = 4
+SHARE = TOK // PARTS
 CUTS = 1
 SIDE = 8
 MODEL = 8
@@ -65,9 +67,10 @@
     act, cot, err4, bkt, sgn, heavy, bkt_s, sgn_s, err, extra, act3, cot3, maps, actb, lhs, hi_a, lo_a, hi_b, lo_b, out, sems, out_sems,
 ):
     pairs = [
-        (bkt_h, bkt), (sgn_h, sgn), (act_h, act), (cot_h, cot),
+        (bkt_h, bkt), (sgn_h, sgn), (act_h.at[:SHARE], act.at[:SHARE]), (cot_h, cot),
         (heavy_h, heavy), (bkt_h, bkt_s), (sgn_h, sgn_s), (err_h, err4),
     ]
+    pairs += [(act_h.at[i * SHARE : (i + 1) * SHARE], act.at[i * SHARE : (i + 1) * SHARE]) for i in range(1, PARTS)]
     copies = [pltpu.make_async_copy(a, b, sems.at[i]) for i, (a, b) in enumerate(pairs)]
     for copy in copies:
         copy.start()
@@ -96,16 +99,25 @@
             at = (r * BUCKETS + b) * KC
             maps[at : at + 2 * KC, :] = jnp.concatenate(two, axis=0).astype(BF16)
 
-    copies[2].wait()
-    for a in range(ROW_BLOCKS):
-        act3[pl.ds(a, TOK, stride=ROW_BLOCKS), :] = act[:, a * BLK : (a + 1) * BLK].astype(F32)
+    def lay(part):
+        for a in range(ROW_BLOCKS):
+            act3[pl.ds(part * SHARE * ROW_BLOCKS + a, SHARE, stride=ROW_BLOCKS), :] = act[
+                part * SHARE : (part + 1) * SHARE, a * BLK : (a + 1) * BLK
+            ].astype(F32)
+        for i in range(part * BLOCKS // PARTS, (part + 1) * BLOCKS // PARTS):
+            for h in range(2):
+                actb[i, :, h * BLK : (h + 1) * BLK] = act3[(2 * i + h) * KIN : (2 * i + h + 1) * KIN, :].astype(BF16)
+
+    for i in range(PARTS):
+        copies[7 + i if i else 2].wait()
+        lay(i)
     copies[3].wait()
     for c in range(COL_BLOCKS):
         cot3[pl.ds(c, TOK, stride=CPAD), :] = cot[:, c * BLK : (c + 1) * BLK].astype(F32)
     cot3[pl.ds(COL_BLOCKS, TOK, stride=CPAD), :] = jnp.zeros((TOK, BLK), F32)
 
     inverse = 1.0 / TOK
-    for copy in copies[5:]:
+    for copy in copies[5:8]:
         copy.wait()
     for r in range(ROWS):
         for j in range(2):
@@ -138,9 +150,6 @@
         extra[j, :HEAVY, :] = guesses
         extra[j, HEAVY:, :] = old
 
-    for i in range(BLOCKS):
-        for h in range(2):
-            actb[i, :, h * BLK : (h + 1) * BLK] = act3[(2 * i + h) * KIN : (2 * i + h + 1) * KIN, :].astype(BF16)
     lhs[...] = cot3[...].T.astype(BF16)
 
     def weigh(g, i, hi, lo):
@@ -231,12 +240,12 @@
             pltpu.VMEM((DEPTH, PAIR * BLK), BF16),
             pltpu.VMEM((DEPTH, PAIR * BLK), BF16),
             pltpu.VMEM((BLK * OUT_ROWS, BLK), F32),
-            pltpu.SemaphoreType.DMA((8,)),
+            pltpu.SemaphoreType.DMA((7 + PARTS,)),
             pltpu.SemaphoreType.DMA((4,)),
         ],
-        compiler_params=pltpu.CompilerParams(vmem_limit_bytes=60 * 1024 * 1024),
+        compiler_params=pltpu.CompilerParams(vmem_limit_bytes=44 * 1024 * 1024),
         name="sketch_block",
-    )(activations, cotangent, error_sketch, bkt, sgn, heavy_blocks)
+    )(*(pltpu.with_memory_space_constraint(x, pltpu.HBM) for x in (activations, cotangent, error_sketch, bkt, sgn, heavy_blocks)))
 
 
 def finish(parts, update, new_error):

time: 61.7 us -> 59 us (0.956)
  Pallas kernels: 9.83 us -> 8.42 us
  blocking collectives: 50.1 us -> 48.9 us
    pallas_call x1, Pallas kernels: 9.19 us -> 7.79 us  [local_part(): pl.pallas_call(kernel, out_shape=jax.ShapeDtypeStruct((4, SIDE // 2, SIDE...]
    all_to_all x1, blocking collectives: 32.7 us -> 31.7 us  [body(): lax.all_to_all(part.reshape(16, 2 * OUT_ROWS, BLK), 'dp', 0, 0, axis_inde...]
where the time goes in v7:
time: 59 us; the launch traced here: 58.1 us
  blocking collectives  48.9 us (83%)
  Pallas kernels  8.42 us (14%)
  between operations  0.64 us (1%)
    all_to_all x1, blocking collectives, body(): lax.all_to_all(part.reshape(16, 2 * OUT_ROWS, BLK), 'dp', 0, 0, axis_inde...  31.7 us
    all_to_all x1, blocking collectives, body(): lax.all_to_all(local.reshape(4, 32 * OUT_ROWS, BLK), ('dp', 'mp'), 0, 0,...  17.2 us
    pallas_call x1, Pallas kernels, local_part(): pl.pallas_call(kernel, out_shape=jax.ShapeDtypeStruct((4, SIDE // 2, SIDE...  7.79 us

profile of v7, /device:TPU:6, one launch (start us, length us, event | category | flops | bytes accessed | tf_op | source)
XLA Modules:
  0.0 58.1 jit_solution(2227297656864580182)
XLA Ops:
  0.6 7.8 %sketch_block.1 = f32[4,4,4,48,128]{4,3,2,1,0:T(8,128)S(1)} custom-call(bf16[128,5120]{1,0:T(8,128)(2,1)} %act_h.1, bf16[128,2176]{1,0:T(8,128)(2,1)} %cot_h.1, f32[1,2,8,256]{3,2,1,0:T(8,128)} %err_h.1, s32[17,2,40]{2,1,0:T(2,128)} %bitcast.6, s32[17,2,40]{2,1,0:T(2,128)} %bitcast.7, s32[8]{0:T(128)} %heavy_h.1), custom_call_target="tpu_custom_call" | custom-call | tf_op jit(solution)/shard_map/sketch_block/pallas_call | solution.py:217
  8.4 17.2 %all_to_all.10 = f32[4,768,128]{2,1,0:T(8,128)S(1)} all-to-all(f32[4,768,128]{2,1,0:T(8,128)S(1)} %bitcast.4), channel_id=1, replica_groups={{0,8,64,72},{1,57,449,505},{2,10,66,74},{3,59,451,507},{4,12,68,76},{5,..., dimensions={0} | all-to-all | bytes 3145728 | tf_op jit(solution)/shard_map/all_to_all | solution.py:279
  25.6 0.1 reduce_sum.9
  25.8 31.7 %all_to_all.11.parts = f32[16,48,128]{2,1,0:T(8,128)S(1)} all-to-all(f32[16,48,128]{2,1,0:T(8,128)S(1)} %bitcast.5), channel_id=1, replica_groups={{0,16,32,48,128,144,160,176,256,272,288,304,384,400,416,432},{8,24,40,5..., dimensions={0} | all-to-all | bytes 786432 | tf_op jit(solution)/shard_map/all_to_all | solution.py:280
  57.4 0.6 %outputs.1 = (f32[1,8,256]{2,1,0:T(8,128)}, f32[1,2,8,256]{3,2,1,0:T(8,128)}) custom-call(f32[16,48,128]{2,1,0:T(8,128)S(1)} %all_to_all.11.parts), custom_call_target="tpu_custom_call" | custom-call | tf_op jit(solution)/shard_map/outputs/pallas_call | solution.py:264

commit v8 on v7

--- a/solution.py
+++ b/solution.py
@@ -42,7 +42,7 @@
     for m in range(MODEL):
         for y in range(SIDE):
             for z in range(SIDE):
-                ys, zs = {y, mate(y, m % 2)}, {z, mate(z, m % 2)}
+                ys, zs = {y, mate(y, 1 - m % 2)}, {z, mate(z, 1 - m % 2)}
                 groups.add(
                     tuple(
                         (u * SIDE + v) * MODEL + m

time: 59 us -> 56.8 us (0.963); the launches traced: 58.1 us -> 56.6 us
  blocking collectives: 48.9 us -> 47.4 us
    all_to_all x1, blocking collectives: 31.7 us -> 19.3 us  [body(): lax.all_to_all(part.reshape(16, 2 * OUT_ROWS, BLK), 'dp', 0, 0, axis_inde...]
    all_to_all x1, blocking collectives: 17.2 us -> 28.2 us  [body(): lax.all_to_all(local.reshape(4, 32 * OUT_ROWS, BLK), ('dp', 'mp'), 0, 0,...]
where the time goes in v8:
time: 56.8 us; the launch traced here: 56.6 us
  blocking collectives  47.4 us (83%)
  Pallas kernels  8.44 us (15%)
  between operations  0.64 us (1%)
    all_to_all x1, blocking collectives, body(): lax.all_to_all(local.reshape(4, 32 * OUT_ROWS, BLK), ('dp', 'mp'), 0, 0,...  28.2 us
    all_to_all x1, blocking collectives, body(): lax.all_to_all(part.reshape(16, 2 * OUT_ROWS, BLK), 'dp', 0, 0, axis_inde...  19.3 us
    pallas_call x1, Pallas kernels, local_part(): pl.pallas_call(kernel, out_shape=jax.ShapeDtypeStruct((4, SIDE // 2, SIDE...  7.8 us

profile of v8, /device:TPU:6, one launch (start us, length us, event | category | flops | bytes accessed | tf_op | source)
XLA Modules:
  0.0 56.6 jit_solution(14234651115025663287)
XLA Ops:
  0.6 7.8 %sketch_block.1 = f32[4,4,4,48,128]{4,3,2,1,0:T(8,128)S(1)} custom-call(bf16[128,5120]{1,0:T(8,128)(2,1)} %act_h.1, bf16[128,2176]{1,0:T(8,128)(2,1)} %cot_h.1, f32[1,2,8,256]{3,2,1,0:T(8,128)} %err_h.1, s32[17,2,40]{2,1,0:T(2,128)} %bitcast.6, s32[17,2,40]{2,1,0:T(2,128)} %bitcast.7, s32[8]{0:T(128)} %heavy_h.1), custom_call_target="tpu_custom_call" | custom-call | tf_op jit(solution)/shard_map/sketch_block/pallas_call | solution.py:217
  8.4 28.2 %all_to_all.10 = f32[4,768,128]{2,1,0:T(8,128)S(1)} all-to-all(f32[4,768,128]{2,1,0:T(8,128)S(1)} %bitcast.4), channel_id=1, replica_groups={{0,56,448,504},{1,9,65,73},{2,58,450,506},{3,11,67,75},{4,60,452,508},{..., dimensions={0} | all-to-all | bytes 3145728 | tf_op jit(solution)/shard_map/all_to_all | solution.py:279
  36.6 0.1 reduce_sum.9
  36.7 19.3 %all_to_all.11.parts = f32[16,48,128]{2,1,0:T(8,128)S(1)} all-to-all(f32[16,48,128]{2,1,0:T(8,128)S(1)} %bitcast.5), channel_id=1, replica_groups={{0,16,32,48,128,144,160,176,256,272,288,304,384,400,416,432},{8,24,40,5..., dimensions={0} | all-to-all | bytes 786432 | tf_op jit(solution)/shard_map/all_to_all | solution.py:280
  56.0 0.6 %outputs.1 = (f32[1,8,256]{2,1,0:T(8,128)}, f32[1,2,8,256]{3,2,1,0:T(8,128)}) custom-call(f32[16,48,128]{2,1,0:T(8,128)S(1)} %all_to_all.11.parts), custom_call_target="tpu_custom_call" | custom-call | tf_op jit(solution)/shard_map/outputs/pallas_call | solution.py:264

commit v9 on v8

--- a/solution.py
+++ b/solution.py
@@ -63,8 +63,8 @@
 
 def kernel(
     act_h, cot_h, err_h, bkt_h, sgn_h, heavy_h,
-    result,
-    act, cot, err4, bkt, sgn, heavy, bkt_s, sgn_s, err, extra, act3, cot3, maps, actb, lhs, hi_a, lo_a, hi_b, lo_b, out, sems, out_sems,
+    out,
+    act, cot, err4, bkt, sgn, heavy, bkt_s, sgn_s, err, extra, act3, cot3, maps, actb, lhs, hi_a, lo_a, hi_b, lo_b, sems,
 ):
     pairs = [
         (bkt_h, bkt), (sgn_h, sgn), (act_h.at[:SHARE], act.at[:SHARE]), (cot_h, cot),
@@ -199,26 +199,15 @@
         at = pl.ds(mine + j * OUT_ROWS, OUT_ROWS)
         out[at, :] = out[at, :] + extra[j]
 
-    whole = out.reshape(SIDE // 2, 2, SIDE // 2, 2, 2 * OUT_ROWS, BLK)
-    sends = [
-        pltpu.make_async_copy(whole.at[:, i, :, j], result.at[2 * i + j], out_sems.at[2 * i + j])
-        for i in range(2)
-        for j in range(2)
-    ]
-    for send in sends:
-        send.start()
-    for send in sends:
-        send.wait()
-
 
 def local_part(activations, cotangent, error_sketch, buckets, sign_bits, heavy_blocks):
     bkt, sgn = buckets.transpose(2, 0, 1), sign_bits.transpose(2, 0, 1)
     hbm = pl.BlockSpec(memory_space=pltpu.HBM)
     return pl.pallas_call(
         kernel,
-        out_shape=jax.ShapeDtypeStruct((4, SIDE // 2, SIDE // 2, 2 * OUT_ROWS, BLK), F32),
+        out_shape=jax.ShapeDtypeStruct((BLK * OUT_ROWS, BLK), F32),
         in_specs=[hbm] * 6,
-        out_specs=hbm,
+        out_specs=pl.BlockSpec(memory_space=pltpu.VMEM),
         scratch_shapes=[
             pltpu.VMEM(activations.shape, BF16),
             pltpu.VMEM(cotangent.shape, BF16),
@@ -239,9 +228,7 @@
             pltpu.VMEM((DEPTH, PAIR * BLK), BF16),
             pltpu.VMEM((DEPTH, PAIR * BLK), BF16),
             pltpu.VMEM((DEPTH, PAIR * BLK), BF16),
-            pltpu.VMEM((BLK * OUT_ROWS, BLK), F32),
             pltpu.SemaphoreType.DMA((7 + PARTS,)),
-            pltpu.SemaphoreType.DMA((4,)),
         ],
         compiler_params=pltpu.CompilerParams(vmem_limit_bytes=44 * 1024 * 1024),
         name="sketch_block",
@@ -276,6 +263,7 @@
 
 def body(activations, cotangent, error_sketch, buckets, sign_bits, heavy_blocks):
     local = local_part(activations, cotangent, error_sketch, buckets, sign_bits, heavy_blocks)
+    local = local.reshape(SIDE // 2, 2, SIDE // 2, 2, 2 * OUT_ROWS, BLK).transpose(1, 3, 0, 2, 4, 5)
     part = lax.all_to_all(local.reshape(4, 32 * OUT_ROWS, BLK), ("dp", "mp"), 0, 0, axis_index_groups=NEAR).sum(axis=0)
     parts = lax.all_to_all(part.reshape(16, 2 * OUT_ROWS, BLK), "dp", 0, 0, axis_index_groups=FAR)
     return outputs(parts)

time: 56.8 us -> 56.8 us (level)
  no operation moved by 1% of the time
where the time goes in v9:
time: 56.8 us; the launch traced here: 56.6 us
  blocking collectives  47.4 us (83%)
  Pallas kernels  8.25 us (15%)
  between operations  0.65 us (1%)
    all_to_all x1, blocking collectives, body(): lax.all_to_all(local.reshape(4, 32 * OUT_ROWS, BLK), ('dp', 'mp'), 0, 0,...  28.2 us
    all_to_all x1, blocking collectives, body(): lax.all_to_all(part.reshape(16, 2 * OUT_ROWS, BLK), 'dp', 0, 0, axis_inde...  19.2 us
    pallas_call x1, Pallas kernels, local_part(): pl.pallas_call(kernel, out_shape=jax.ShapeDtypeStruct((BLK * OUT_ROWS, BL...  7.61 us

profile of v9, /device:TPU:6, one launch (start us, length us, event | category | flops | bytes accessed | tf_op | source)
XLA Modules:
  0.0 56.6 jit_solution(18341408721779981249)
XLA Ops:
  0.6 7.6 %sketch_block.1 = f32[3072,128]{1,0:T(8,128)S(1)} custom-call(bf16[128,5120]{1,0:T(8,128)(2,1)} %act_h.1, bf16[128,2176]{1,0:T(8,128)(2,1)} %cot_h.1, f32[1,2,8,256]{3,2,1,0:T(8,128)} %err_h.1, s32[17,2,40]{2,1,0:T(2,128)} %bitcast.10, s32[17,2,40]{2,1,0:T(2,128)} %bitcast.11, s32[8]{0:T(128)} %heavy_h.1), custom_call_target="tpu_custom_call" | custom-call | tf_op jit(solution)/shard_map/sketch_block/pallas_call | solution.py:206
  8.3 0.2 copy.8
  8.4 28.2 %all_to_all.10 = f32[4,768,128]{2,1,0:T(8,128)S(1)} all-to-all(f32[4,768,128]{2,1,0:T(8,128)S(1)} %bitcast.8), channel_id=1, replica_groups={{0,56,448,504},{1,9,65,73},{2,58,450,506},{3,11,67,75},{4,60,452,508},{..., dimensions={0} | all-to-all | bytes 3145728 | tf_op jit(solution)/shard_map/all_to_all | solution.py:267
  36.6 0.1 reduce_sum.9
  36.7 19.2 %all_to_all.11.parts = f32[16,48,128]{2,1,0:T(8,128)S(1)} all-to-all(f32[16,48,128]{2,1,0:T(8,128)S(1)} %bitcast.9), channel_id=1, replica_groups={{0,16,32,48,128,144,160,176,256,272,288,304,384,400,416,432},{8,24,40,5..., dimensions={0} | all-to-all | bytes 786432 | tf_op jit(solution)/shard_map/all_to_all | solution.py:268
  56.0 0.6 %outputs.1 = (f32[1,8,256]{2,1,0:T(8,128)}, f32[1,2,8,256]{3,2,1,0:T(8,128)}) custom-call(f32[16,48,128]{2,1,0:T(8,128)S(1)} %all_to_all.11.parts), custom_call_target="tpu_custom_call" | custom-call | tf_op jit(solution)/shard_map/outputs/pallas_call | solution.py:251
